TPU v7x, 32 devices: a whole 2x2x4 slice. The times are simulated.
32 devices in a mesh: section: 4 (over x, core), dp: 8 (over z, y).
Axes of the slice: x: 2, y: 2, z: 4, core: 2. Of those that a mesh axis runs over, the one named last changes fastest.
Arguments:
- stack_input: bfloat16 [1024, 12288], P('dp'), may hold values from -6 to 6
- out_cotangent: bfloat16 [1024, 12288], P('dp'), may hold values from -6 to 6
- norm_gain: float32 [4, 12288], P('section'), may hold values from 0.5 to 1.5
- master_in: float32 [4, 12288, 128], P('section', 'dp'), may hold values from -0.0546875 to 0.0546875
- master_out: float32 [4, 128, 12288], P('section', None, 'dp'), may hold values from -0.5 to 0.5
- first_in: float32 [4, 12288, 128], P('section', 'dp'), may hold values from -3 to 3
- first_out: float32 [4, 128, 12288], P('section', None, 'dp'), may hold values from -0.1 to 0.1
- second_in: float32 [4, 12288, 128], P('section', 'dp'), may hold values from 0.02 to 0.5
- second_out: float32 [4, 128, 12288], P('section', None, 'dp'), may hold values from 0.02 to 0.5
Outputs:
- section_outputs: bfloat16 [4, 1024, 12288], P('section', 'dp')
- new_master_in: float32 [4, 12288, 128], P('section', 'dp')
- new_master_out: float32 [4, 128, 12288], P('section', None, 'dp')
- new_first_in: float32 [4, 12288, 128], P('section', 'dp')
- new_first_out: float32 [4, 128, 12288], P('section', None, 'dp')
- new_second_in: float32 [4, 12288, 128], P('section', 'dp')
- new_second_out: float32 [4, 128, 12288], P('section', None, 'dp')
All inputs are finite; a program needn't handle non-finite values.
Results may differ from a plain program's by a relative error of at most 0.018.
Values may be sent and summed in bfloat16 or wider, within the bound.
A program may use at most 128 MiB of HBM per device.

v0:
```python
import math

import jax
import jax.numpy as jnp
from jax import lax
from jax.sharding import PartitionSpec as P

MICRO = 4
STEP = 10


norm_eps = 1e-05
gelu_coef = 0.7978845608028654
beta_one = 0.9
beta_two = 0.95
adam_eps = 1e-08
learn_rate = 0.05
decay_rate = 0.1
clip_rms = 0.5


def passed_along(block, axis, distance):
    devices = range(lax.axis_size(axis))
    route = [(i - distance, i) for i in devices if i - distance in devices]
    return lax.ppermute(block, axis, route)


def gelu_pair(hidden_pre):
    inner_arg = gelu_coef * (hidden_pre + 0.044715 * hidden_pre * hidden_pre * hidden_pre)
    tangent = jnp.tanh(inner_arg)
    gelu_value = 0.5 * hidden_pre * (1.0 + tangent)
    gelu_slope = 0.5 * (1.0 + tangent) + 0.5 * hidden_pre * (
        1.0 - tangent * tangent
    ) * gelu_coef * (1.0 + 3.0 * 0.044715 * hidden_pre * hidden_pre)
    return (gelu_value, gelu_slope)


def contract_rows(left_arr, right_arr):
    return lax.dot_general(
        left_arr, right_arr, (((0,), (0,)), ((), ())), preferred_element_type=jnp.float32
    )


def contract_last(left_arr, right_arr):
    return lax.dot_general(
        left_arr, right_arr, (((1,), (1,)), ((), ())), preferred_element_type=jnp.float32
    )


def norm_parts(inputs, gain_row):
    wide_input = inputs.astype(jnp.float32)
    inv_rms = lax.rsqrt(jnp.mean(wide_input * wide_input, axis=-1, keepdims=True) + norm_eps)
    normed = (wide_input * inv_rms * gain_row).astype(jnp.bfloat16)
    return (wide_input, inv_rms, normed)


def layer_forward(inputs, gain_row, weight_in, weight_out):
    wide_input, inv_rms, normed = norm_parts(inputs, gain_row)
    hidden_pre = jnp.dot(normed, weight_in, preferred_element_type=jnp.float32)
    gelu_value, gelu_slope = gelu_pair(hidden_pre)
    act_low = gelu_value.astype(jnp.bfloat16)
    result = (wide_input + jnp.dot(act_low, weight_out, preferred_element_type=jnp.float32)).astype(
        jnp.bfloat16
    )
    return (result, hidden_pre)


def layer_backward(inputs, gain_row, weight_in, weight_out, hidden_pre, incoming):
    wide_input, inv_rms, normed = norm_parts(inputs, gain_row)
    gelu_value, gelu_slope = gelu_pair(hidden_pre)
    act_low = gelu_value.astype(jnp.bfloat16)
    d_act = contract_last(incoming, weight_out)
    d_pre = (d_act * gelu_slope).astype(jnp.bfloat16)
    scaled = contract_last(d_pre, weight_in) * gain_row
    d_inputs = (
        incoming.astype(jnp.float32)
        + inv_rms * scaled
        - wide_input * inv_rms**3 * jnp.mean(wide_input * scaled, axis=-1, keepdims=True)
    )
    return (d_inputs.astype(jnp.bfloat16), d_pre, act_low, normed)


def adam_update(master, first, second, grad):
    first_new = beta_one * first + (1.0 - beta_one) * grad
    second_new = beta_two * second + (1.0 - beta_two) * grad * grad
    first_hat = first_new / (1.0 - beta_one**STEP)
    second_hat = second_new / (1.0 - beta_two**STEP)
    master_new = master - learn_rate * (
        first_hat / (jnp.sqrt(second_hat) + adam_eps) + decay_rate * master
    )
    return (master_new, first_new, second_new)


def store_block(buffer, values, slot_pos, in_range):
    old_block = lax.dynamic_index_in_dim(buffer, slot_pos, 0, keepdims=False)
    return lax.dynamic_update_index_in_dim(
        buffer, jnp.where(in_range, values, old_block), slot_pos, 0
    )


def shards(
    stack_input,
    out_cotangent,
    norm_gain,
    master_in,
    master_out,
    first_in,
    first_out,
    second_in,
    second_out,
):
    num_sections = lax.axis_size("section")
    section_pos = lax.axis_index("section")
    gain_row = norm_gain[0]
    work_in, work_out = (
        lax.all_gather(master_in[0].astype(jnp.bfloat16), "dp", axis=0, tiled=True),
        lax.all_gather(master_out[0].astype(jnp.bfloat16), "dp", axis=1, tiled=True),
    )
    tok_rows = stack_input.shape[0]
    model_width = stack_input.shape[1]
    rank_width = work_in.shape[1]
    num_blocks = MICRO
    block_rows = tok_rows // num_blocks
    num_ticks = num_sections + num_blocks - 1
    input_blocks = stack_input.reshape(num_blocks, block_rows, model_width)
    cot_blocks = out_cotangent.reshape(num_blocks, block_rows, model_width)
    accumulate = False
    accumulate = True
    zero_rows = jnp.zeros((block_rows, model_width), jnp.bfloat16)
    zero_pre_rows = jnp.zeros((block_rows, rank_width), jnp.float32)

    def forward_tick(tick_num, loop_state):
        arriving, kept_inputs, kept_pre, produced = loop_state
        block_pos = tick_num - section_pos
        in_range = (block_pos >= 0) & (block_pos < num_blocks)
        slot_pos = jnp.clip(block_pos, 0, num_blocks - 1)
        first_rows = lax.dynamic_index_in_dim(input_blocks, slot_pos, 0, keepdims=False)
        current = jnp.where(section_pos == 0, first_rows, arriving)

        def forward_run_layer(operand):
            return layer_forward(operand, gain_row, work_in, work_out)

        def forward_skip_layer(operand):
            return (zero_rows, zero_pre_rows)

        result, hidden_pre = lax.cond(in_range, forward_run_layer, forward_skip_layer, current)
        kept_inputs = store_block(kept_inputs, current, slot_pos, in_range)
        kept_pre = store_block(kept_pre, hidden_pre, slot_pos, in_range)
        produced = store_block(produced, result, slot_pos, in_range)
        arriving = passed_along(result, "section", 1)
        return (arriving, kept_inputs, kept_pre, produced)

    zero_blocks = jnp.zeros((num_blocks, block_rows, model_width), jnp.bfloat16)
    zero_pre = jnp.zeros((num_blocks, block_rows, rank_width), jnp.float32)
    arriving, kept_inputs, kept_pre, produced = lax.fori_loop(
        0, num_ticks, forward_tick, (zero_rows, zero_blocks, zero_pre, zero_blocks)
    )
    zero_rank_rows = jnp.zeros((block_rows, rank_width), jnp.bfloat16)

    def backward_tick(tick_num, loop_state):
        arriving, acc_in, acc_out, kept_normed, kept_dpre, kept_act, kept_delta = loop_state
        block_pos = tick_num - (num_sections - 1 - section_pos)
        in_range = (block_pos >= 0) & (block_pos < num_blocks)
        slot_pos = jnp.clip(block_pos, 0, num_blocks - 1)
        last_rows = lax.dynamic_index_in_dim(cot_blocks, slot_pos, 0, keepdims=False)
        incoming = jnp.where(section_pos == num_sections - 1, last_rows, arriving)
        current = lax.dynamic_index_in_dim(kept_inputs, slot_pos, 0, keepdims=False)
        hidden_pre = lax.dynamic_index_in_dim(kept_pre, slot_pos, 0, keepdims=False)

        def backward_run_layer(operands):
            acc_first, acc_second = operands
            d_inputs, d_pre, act_low, normed = layer_backward(
                current, gain_row, work_in, work_out, hidden_pre, incoming
            )
            acc_first = acc_first + contract_rows(normed, d_pre)
            acc_second = acc_second + contract_rows(act_low, incoming)
            return (d_inputs, d_pre, act_low, normed, acc_first, acc_second)

        def backward_skip_layer(operands):
            acc_first, acc_second = operands
            return (zero_rows, zero_rank_rows, zero_rank_rows, zero_rows, acc_first, acc_second)

        d_inputs, d_pre, act_low, normed, acc_in, acc_out = lax.cond(
            in_range, backward_run_layer, backward_skip_layer, (acc_in, acc_out)
        )
        arriving = passed_along(d_inputs, "section", -1)
        return (arriving, acc_in, acc_out, kept_normed, kept_dpre, kept_act, kept_delta)

    acc_shape_in = (model_width, rank_width)
    acc_shape_out = (rank_width, model_width)
    keep_blocks = 1
    start_state = (
        zero_rows,
        jnp.zeros(acc_shape_in, jnp.float32),
        jnp.zeros(acc_shape_out, jnp.float32),
        jnp.zeros((keep_blocks, block_rows, model_width), jnp.bfloat16),
        jnp.zeros((keep_blocks, block_rows, rank_width), jnp.bfloat16),
        jnp.zeros((keep_blocks, block_rows, rank_width), jnp.bfloat16),
        jnp.zeros((keep_blocks, block_rows, model_width), jnp.bfloat16),
    )
    final_state = lax.fori_loop(0, num_ticks, backward_tick, start_state)
    acc_in, acc_out, kept_normed, kept_dpre, kept_act, kept_delta = final_state[1:]
    full_in, full_out = (acc_in, acc_out)
    shard_in, shard_out = (
        lax.psum_scatter(full_in, "dp", scatter_dimension=0, tiled=True),
        lax.psum_scatter(full_out, "dp", scatter_dimension=1, tiled=True),
    )
    local_sq = jnp.sum(shard_in * shard_in) + jnp.sum(shard_out * shard_out)
    total_sq = lax.psum(local_sq, ("section", "dp"))
    norm_limit = clip_rms * math.sqrt(2.0 * model_width * rank_width * num_sections)
    clip_factor = norm_limit / jnp.maximum(jnp.sqrt(total_sq), norm_limit)
    new_in, new_first_in, new_second_in = adam_update(
        master_in[0], first_in[0], second_in[0], clip_factor * shard_in
    )
    new_out, new_first_out, new_second_out = adam_update(
        master_out[0], first_out[0], second_out[0], clip_factor * shard_out
    )
    section_rows = produced.reshape(1, tok_rows, model_width)
    return (
        section_rows,
        new_in[None],
        new_out[None],
        new_first_in[None],
        new_first_out[None],
        new_second_in[None],
        new_second_out[None],
    )


def solution(mesh):
    in_specs = (
        P("dp", None),
        P("dp", None),
        P("section", None),
        P("section", "dp", None),
        P("section", None, "dp"),
        P("section", "dp", None),
        P("section", None, "dp"),
        P("section", "dp", None),
        P("section", None, "dp"),
    )
    out_specs = (
        P("section", "dp", None),
        P("section", "dp", None),
        P("section", None, "dp"),
        P("section", "dp", None),
        P("section", None, "dp"),
        P("section", "dp", None),
        P("section", None, "dp"),
    )
    return jax.shard_map(shards, mesh=mesh, in_specs=in_specs, out_specs=out_specs, check_vma=False)
```

profile of v0, /device:TPU:0, one launch (start us, length us, event | category | flops | bytes accessed | tf_op | source)
XLA Modules:
  0.0 751.0 jit_solution(13861671391485237756)
XLA Ops:
  11.2 62.7 %all-gather.3.cloned.1.call-done = bf16[12288,128]{1,0:T(8,128)(2,1)} async-done(((bf16[1536,128]{1,0:T(8,128)(2,1)}), bf16[12288,128]{1,0:T(8,128)(2,1)}) %all-gather.3.cloned.1.call-update) | async-done | bytes 3145744 | tf_op jit(solution)/shard_map/all_gather | solution.py:116
  73.9 61.9 %all-gather.5.cloned.1.call-done = bf16[128,12288]{1,0:T(8,128)(2,1)} async-done(((bf16[128,1536]{1,0:T(8,128)(2,1)}), bf16[128,12288]{1,0:T(8,128)(2,1)}) %all-gather.5.cloned.1.call-update) | async-done | bytes 3145744 | tf_op jit(solution)/shard_map/all_gather | solution.py:117
  140.8 132.7 %while.39 = (s32[]{:T(128)}, bf16[32,12288]{1,0:T(8,128)(2,1)}, bf16[4,32,12288]{2,1,0:T(8,128)(2,1)}, f32[4,32,128]{2,1,0:T(8,128)S(1)}, bf16[4,32,12288]{2,1,0...) while((s32[]{:T(128)}, bf16[32,12288]{1,0:T(8,128)(2,1)}, ...), condition=%wide.region_4.5_spmd, body=%wide.region_0.4_spmd.sunk | while | flops 206479392 | bytes 34768216 | solution.py:155
  142.1 2.4 bitcast_dynamic-update-slice_fusion.6
  144.5 3.7 conditional.4
  151.5 2.2 bitcast_dynamic-update-slice_fusion.8
  155.8 2.4 bitcast_dynamic-update-slice_fusion.6
  158.2 3.7 conditional.4
  161.9 7.5 %collective-permute-start = (bf16[32,12288]{1,0:T(8,128)(2,1)}, bf16[32,12288]{1,0:T(8,128)(2,1)}, u32[]{:S(2)}, u32[]{:S(2)}) collective-permute-start(bf16[32,12288]{1,0:T(8,128)(2,1)} %get-tuple-element.839), channel_id=1, source_target_pairs={{0,8},{8,16},{16,24},{1,9},{9,17},{17,25},{2,10},{10,18},{18,26},{... | collective-permute-start | bytes 2359304 | tf_op jit(solution)/shard_map/while/body/eval_jaxpr/ppermute | solution.py:25
  170.6 2.2 bitcast_dynamic-update-slice_fusion.8
  174.8 2.3 bitcast_dynamic-update-slice_fusion.6
  177.2 3.7 conditional.4
  180.9 7.6 %collective-permute-start = (bf16[32,12288]{1,0:T(8,128)(2,1)}, bf16[32,12288]{1,0:T(8,128)(2,1)}, u32[]{:S(2)}, u32[]{:S(2)}) collective-permute-start(bf16[32,12288]{1,0:T(8,128)(2,1)} %get-tuple-element.839), channel_id=1, source_target_pairs={{0,8},{8,16},{16,24},{1,9},{9,17},{17,25},{2,10},{10,18},{18,26},{... | collective-permute-start | bytes 2359304 | tf_op jit(solution)/shard_map/while/body/eval_jaxpr/ppermute | solution.py:25
  193.9 2.3 bitcast_dynamic-update-slice_fusion.6
  196.3 3.7 conditional.4
  200.0 9.7 %collective-permute-start = (bf16[32,12288]{1,0:T(8,128)(2,1)}, bf16[32,12288]{1,0:T(8,128)(2,1)}, u32[]{:S(2)}, u32[]{:S(2)}) collective-permute-start(bf16[32,12288]{1,0:T(8,128)(2,1)} %get-tuple-element.839), channel_id=1, source_target_pairs={{0,8},{8,16},{16,24},{1,9},{9,17},{17,25},{2,10},{10,18},{18,26},{... | collective-permute-start | bytes 2359304 | tf_op jit(solution)/shard_map/while/body/eval_jaxpr/ppermute | solution.py:25
  215.1 2.3 bitcast_dynamic-update-slice_fusion.6
  219.0 11.9 %collective-permute-start = (bf16[32,12288]{1,0:T(8,128)(2,1)}, bf16[32,12288]{1,0:T(8,128)(2,1)}, u32[]{:S(2)}, u32[]{:S(2)}) collective-permute-start(bf16[32,12288]{1,0:T(8,128)(2,1)} %get-tuple-element.839), channel_id=1, source_target_pairs={{0,8},{8,16},{16,24},{1,9},{9,17},{17,25},{2,10},{10,18},{18,26},{... | collective-permute-start | bytes 2359304 | tf_op jit(solution)/shard_map/while/body/eval_jaxpr/ppermute | solution.py:25
  234.6 2.3 bitcast_dynamic-update-slice_fusion.6
  238.5 11.5 %collective-permute-start = (bf16[32,12288]{1,0:T(8,128)(2,1)}, bf16[32,12288]{1,0:T(8,128)(2,1)}, u32[]{:S(2)}, u32[]{:S(2)}) collective-permute-start(bf16[32,12288]{1,0:T(8,128)(2,1)} %get-tuple-element.839), channel_id=1, source_target_pairs={{0,8},{8,16},{16,24},{1,9},{9,17},{17,25},{2,10},{10,18},{18,26},{... | collective-permute-start | bytes 2359304 | tf_op jit(solution)/shard_map/while/body/eval_jaxpr/ppermute | solution.py:25
  253.6 2.3 bitcast_dynamic-update-slice_fusion.6
  257.5 13.7 %collective-permute-start = (bf16[32,12288]{1,0:T(8,128)(2,1)}, bf16[32,12288]{1,0:T(8,128)(2,1)}, u32[]{:S(2)}, u32[]{:S(2)}) collective-permute-start(bf16[32,12288]{1,0:T(8,128)(2,1)} %get-tuple-element.839), channel_id=1, source_target_pairs={{0,8},{8,16},{16,24},{1,9},{9,17},{17,25},{2,10},{10,18},{18,26},{... | collective-permute-start | bytes 2359304 | tf_op jit(solution)/shard_map/while/body/eval_jaxpr/ppermute | solution.py:25
  274.4 3.3 broadcast_in_dim.75
  277.7 2.9 broadcast_in_dim.74
  280.6 174.2 %while.40 = (s32[]{:T(128)}, bf16[32,12288]{1,0:T(8,128)(2,1)}, f32[12288,128]{1,0:T(8,128)}, f32[128,12288]{1,0:T(8,128)}, s32[]{:T(128)}, /*index=5*/pred[]{:T...) while((s32[]{:T(128)}, bf16[32,12288]{1,0:T(8,128)(2,1)}, ...), condition=%wide.region_10.11_spmd, body=%wide.region_5.10_spmd.sunk | while | flops 413384800 | bytes 146434384 | solution.py:201
  282.8 11.2 %collective-permute-done.1 = bf16[32,12288]{1,0:T(8,128)(2,1)} collective-permute-done((bf16[32,12288]{1,0:T(8,128)(2,1)}, bf16[32,12288]{1,0:T(8,128)(2,1)}, u32[]{:S(2)}, u32[]{:S(2)}) %collective-permute-start.1) | collective-permute-done | bytes 786464 | tf_op jit(solution)/shard_map/while/body/eval_jaxpr/ppermute | solution.py:25
  296.2 13.1 %collective-permute-done.1 = bf16[32,12288]{1,0:T(8,128)(2,1)} collective-permute-done((bf16[32,12288]{1,0:T(8,128)(2,1)}, bf16[32,12288]{1,0:T(8,128)(2,1)}, u32[]{:S(2)}, u32[]{:S(2)}) %collective-permute-start.1) | collective-permute-done | bytes 786464 | tf_op jit(solution)/shard_map/while/body/eval_jaxpr/ppermute | solution.py:25
  311.5 38.3 %collective-permute-done.1 = bf16[32,12288]{1,0:T(8,128)(2,1)} collective-permute-done((bf16[32,12288]{1,0:T(8,128)(2,1)}, bf16[32,12288]{1,0:T(8,128)(2,1)}, u32[]{:S(2)}, u32[]{:S(2)}) %collective-permute-start.1) | collective-permute-done | bytes 786464 | tf_op jit(solution)/shard_map/while/body/eval_jaxpr/ppermute | solution.py:25
  349.9 14.9 %conditional.5 = (bf16[32,12288]{1,0:T(8,128)(2,1)}, f32[12288,128]{1,0:T(8,128)}, f32[128,12288]{1,0:T(8,128)}) conditional(s32[]{:T(128)} %convert_element_type.104, (f32[12288,128]{1,0:T(8,128)}, f32[128,12288]{1,0:T(8,128)}) %tuple.108, (pred[]{:T(512)}, s32[]{:T(128)}, bf16[4,32,12288]{2,1,0:T(8,128)(2,1)}, bf16[32,12288]{1,0:T(8,128)(2,1)}, ...), branch_computations={%region_6.6_spmd, %region_7.9_spmd} | conditional | flops 413384800 | bytes 143288320 | solution.py:183
  351.5 3.2 fusion.29
  362.1 2.6 copy-done.3
  366.0 12.3 %collective-permute-done.1 = bf16[32,12288]{1,0:T(8,128)(2,1)} collective-permute-done((bf16[32,12288]{1,0:T(8,128)(2,1)}, bf16[32,12288]{1,0:T(8,128)(2,1)}, u32[]{:S(2)}, u32[]{:S(2)}) %collective-permute-start.1) | collective-permute-done | bytes 786464 | tf_op jit(solution)/shard_map/while/body/eval_jaxpr/ppermute | solution.py:25
  378.4 14.9 %conditional.5 = (bf16[32,12288]{1,0:T(8,128)(2,1)}, f32[12288,128]{1,0:T(8,128)}, f32[128,12288]{1,0:T(8,128)}) conditional(s32[]{:T(128)} %convert_element_type.104, (f32[12288,128]{1,0:T(8,128)}, f32[128,12288]{1,0:T(8,128)}) %tuple.108, (pred[]{:T(512)}, s32[]{:T(128)}, bf16[4,32,12288]{2,1,0:T(8,128)(2,1)}, bf16[32,12288]{1,0:T(8,128)(2,1)}, ...), branch_computations={%region_6.6_spmd, %region_7.9_spmd} | conditional | flops 413384800 | bytes 143288320 | solution.py:183
  380.0 3.2 fusion.29
  390.6 2.6 copy-done.3
  394.5 12.3 %collective-permute-done.1 = bf16[32,12288]{1,0:T(8,128)(2,1)} collective-permute-done((bf16[32,12288]{1,0:T(8,128)(2,1)}, bf16[32,12288]{1,0:T(8,128)(2,1)}, u32[]{:S(2)}, u32[]{:S(2)}) %collective-permute-start.1) | collective-permute-done | bytes 786464 | tf_op jit(solution)/shard_map/while/body/eval_jaxpr/ppermute | solution.py:25
  406.9 14.9 %conditional.5 = (bf16[32,12288]{1,0:T(8,128)(2,1)}, f32[12288,128]{1,0:T(8,128)}, f32[128,12288]{1,0:T(8,128)}) conditional(s32[]{:T(128)} %convert_element_type.104, (f32[12288,128]{1,0:T(8,128)}, f32[128,12288]{1,0:T(8,128)}) %tuple.108, (pred[]{:T(512)}, s32[]{:T(128)}, bf16[4,32,12288]{2,1,0:T(8,128)(2,1)}, bf16[32,12288]{1,0:T(8,128)(2,1)}, ...), branch_computations={%region_6.6_spmd, %region_7.9_spmd} | conditional | flops 413384800 | bytes 143288320 | solution.py:183
  408.5 3.2 fusion.29
  419.1 2.6 copy-done.3
  423.0 12.3 %collective-permute-done.1 = bf16[32,12288]{1,0:T(8,128)(2,1)} collective-permute-done((bf16[32,12288]{1,0:T(8,128)(2,1)}, bf16[32,12288]{1,0:T(8,128)(2,1)}, u32[]{:S(2)}, u32[]{:S(2)}) %collective-permute-start.1) | collective-permute-done | bytes 786464 | tf_op jit(solution)/shard_map/while/body/eval_jaxpr/ppermute | solution.py:25
  435.4 14.9 %conditional.5 = (bf16[32,12288]{1,0:T(8,128)(2,1)}, f32[12288,128]{1,0:T(8,128)}, f32[128,12288]{1,0:T(8,128)}) conditional(s32[]{:T(128)} %convert_element_type.104, (f32[12288,128]{1,0:T(8,128)}, f32[128,12288]{1,0:T(8,128)}) %tuple.108, (pred[]{:T(512)}, s32[]{:T(128)}, bf16[4,32,12288]{2,1,0:T(8,128)(2,1)}, bf16[32,12288]{1,0:T(8,128)(2,1)}, ...), branch_computations={%region_6.6_spmd, %region_7.9_spmd} | conditional | flops 413384800 | bytes 143288320 | solution.py:183
  437.0 3.2 fusion.29
  447.6 2.6 copy-done.3
  451.5 3.2 collective-permute-done.1
  455.3 119.7 %reduce-scatter.3.cloned.1.call-done = f32[1536,128]{1,0:T(8,128)} async-done(((f32[12288,128]{1,0:T(8,128)}), f32[1536,128]{1,0:T(8,128)}) %reduce-scatter.3.cloned.1.call-update) | async-done | bytes 786448 | tf_op jit(solution)/shard_map/reduce_scatter | solution.py:205
  576.9 118.6 %reduce-scatter.5.cloned.1.call-done = f32[128,1536]{1,0:T(8,128)} async-done(((f32[128,12288]{1,0:T(8,128)}), f32[128,1536]{1,0:T(8,128)}) %reduce-scatter.5.cloned.1.call-update) | async-done | bytes 786448 | tf_op jit(solution)/shard_map/reduce_scatter | solution.py:206
  698.8 39.4 %psum.7 = f32[]{:T(128)} all-reduce(f32[]{:T(128)S(6)} %add.169), channel_id=1, replica_groups=mesh['section'=4,'dp'=8] {'section','dp'}, use_global_device_ids=true, to_apply=%region_15.16 | all-reduce | flops 1 | bytes 8 | tf_op jit(solution)/shard_map/psum | solution.py:209
  739.0 3.5 fusion.60
  (211 shorter events, 121.0 us)
Async XLA Ops:
  7.2 66.8 %all-gather.3.cloned.1.call-start = ((), (), s32[]{:S(2)}) async-start(), calls=%async_computation.2 | async-start | bytes 3538944 | tf_op jit(solution)/shard_map/all_gather | solution.py:116
  9.2 126.7 %all-gather.5.cloned.1.call-start = ((), (), s32[]{:S(2)}) async-start(), calls=%async_computation.3 | async-start | bytes 3538944 | tf_op jit(solution)/shard_map/all_gather | solution.py:117
  11.2 563.8 %reduce-scatter.3.cloned.1.call-start = ((), (), s32[]{:S(2)}) async-start(), calls=%async_computation.4 | async-start | bytes 7077888 | tf_op jit(solution)/shard_map/reduce_scatter | solution.py:205
  136.8 3.9 copy-start
  136.8 3.9 copy-start.5
  140.8 3.7 copy-start.1
  148.2 6.3 collective-permute-start
  154.5 3.7 copy-start.1
  161.9 11.6 %collective-permute-start = (bf16[32,12288]{1,0:T(8,128)(2,1)}, bf16[32,12288]{1,0:T(8,128)(2,1)}, u32[]{:S(2)}, u32[]{:S(2)}) collective-permute-start(bf16[32,12288]{1,0:T(8,128)(2,1)} %get-tuple-element.839), channel_id=1, source_target_pairs={{0,8},{8,16},{16,24},{1,9},{9,17},{17,25},{2,10},{10,18},{18,26},{... | collective-permute-start | bytes 2359304 | tf_op jit(solution)/shard_map/while/body/eval_jaxpr/ppermute | solution.py:25
  173.5 3.7 copy-start.1
  180.9 11.7 %collective-permute-start = (bf16[32,12288]{1,0:T(8,128)(2,1)}, bf16[32,12288]{1,0:T(8,128)(2,1)}, u32[]{:S(2)}, u32[]{:S(2)}) collective-permute-start(bf16[32,12288]{1,0:T(8,128)(2,1)} %get-tuple-element.839), channel_id=1, source_target_pairs={{0,8},{8,16},{16,24},{1,9},{9,17},{17,25},{2,10},{10,18},{18,26},{... | collective-permute-start | bytes 2359304 | tf_op jit(solution)/shard_map/while/body/eval_jaxpr/ppermute | solution.py:25
  192.6 3.7 copy-start.1
  200.0 13.8 %collective-permute-start = (bf16[32,12288]{1,0:T(8,128)(2,1)}, bf16[32,12288]{1,0:T(8,128)(2,1)}, u32[]{:S(2)}, u32[]{:S(2)}) collective-permute-start(bf16[32,12288]{1,0:T(8,128)(2,1)} %get-tuple-element.839), channel_id=1, source_target_pairs={{0,8},{8,16},{16,24},{1,9},{9,17},{17,25},{2,10},{10,18},{18,26},{... | collective-permute-start | bytes 2359304 | tf_op jit(solution)/shard_map/while/body/eval_jaxpr/ppermute | solution.py:25
  213.8 3.7 copy-start.1
  219.0 14.2 %collective-permute-start = (bf16[32,12288]{1,0:T(8,128)(2,1)}, bf16[32,12288]{1,0:T(8,128)(2,1)}, u32[]{:S(2)}, u32[]{:S(2)}) collective-permute-start(bf16[32,12288]{1,0:T(8,128)(2,1)} %get-tuple-element.839), channel_id=1, source_target_pairs={{0,8},{8,16},{16,24},{1,9},{9,17},{17,25},{2,10},{10,18},{18,26},{... | collective-permute-start | bytes 2359304 | tf_op jit(solution)/shard_map/while/body/eval_jaxpr/ppermute | solution.py:25
  233.2 3.7 copy-start.1
  238.5 13.8 %collective-permute-start = (bf16[32,12288]{1,0:T(8,128)(2,1)}, bf16[32,12288]{1,0:T(8,128)(2,1)}, u32[]{:S(2)}, u32[]{:S(2)}) collective-permute-start(bf16[32,12288]{1,0:T(8,128)(2,1)} %get-tuple-element.839), channel_id=1, source_target_pairs={{0,8},{8,16},{16,24},{1,9},{9,17},{17,25},{2,10},{10,18},{18,26},{... | collective-permute-start | bytes 2359304 | tf_op jit(solution)/shard_map/while/body/eval_jaxpr/ppermute | solution.py:25
  252.3 3.7 copy-start.1
  257.5 15.9 %collective-permute-start = (bf16[32,12288]{1,0:T(8,128)(2,1)}, bf16[32,12288]{1,0:T(8,128)(2,1)}, u32[]{:S(2)}, u32[]{:S(2)}) collective-permute-start(bf16[32,12288]{1,0:T(8,128)(2,1)} %get-tuple-element.839), channel_id=1, source_target_pairs={{0,8},{8,16},{16,24},{1,9},{9,17},{17,25},{2,10},{10,18},{18,26},{... | collective-permute-start | bytes 2359304 | tf_op jit(solution)/shard_map/while/body/eval_jaxpr/ppermute | solution.py:25
  281.5 12.5 %collective-permute-start.1 = (bf16[32,12288]{1,0:T(8,128)(2,1)}, bf16[32,12288]{1,0:T(8,128)(2,1)}, u32[]{:S(2)}, u32[]{:S(2)}) collective-permute-start(bf16[32,12288]{1,0:T(8,128)(2,1)} %get-tuple-element.854), channel_id=1, source_target_pairs={{8,0},{16,8},{24,16},{9,1},{17,9},{25,17},{10,2},{18,10},{26,18},{... | collective-permute-start | bytes 2359304 | tf_op jit(solution)/shard_map/while/body/eval_jaxpr/ppermute | solution.py:25
  295.0 14.4 %collective-permute-start.1 = (bf16[32,12288]{1,0:T(8,128)(2,1)}, bf16[32,12288]{1,0:T(8,128)(2,1)}, u32[]{:S(2)}, u32[]{:S(2)}) collective-permute-start(bf16[32,12288]{1,0:T(8,128)(2,1)} %get-tuple-element.854), channel_id=1, source_target_pairs={{8,0},{16,8},{24,16},{9,1},{17,9},{25,17},{10,2},{18,10},{26,18},{... | collective-permute-start | bytes 2359304 | tf_op jit(solution)/shard_map/while/body/eval_jaxpr/ppermute | solution.py:25
  310.2 39.6 %collective-permute-start.1 = (bf16[32,12288]{1,0:T(8,128)(2,1)}, bf16[32,12288]{1,0:T(8,128)(2,1)}, u32[]{:S(2)}, u32[]{:S(2)}) collective-permute-start(bf16[32,12288]{1,0:T(8,128)(2,1)} %get-tuple-element.854), channel_id=1, source_target_pairs={{8,0},{16,8},{24,16},{9,1},{17,9},{25,17},{10,2},{18,10},{26,18},{... | collective-permute-start | bytes 2359304 | tf_op jit(solution)/shard_map/while/body/eval_jaxpr/ppermute | solution.py:25
  349.9 4.9 copy-start.4
  351.5 5.9 slice-start
  354.7 2.7 slice-start.1
  356.1 3.4 slice-start.2
  364.7 13.6 %collective-permute-start.1 = (bf16[32,12288]{1,0:T(8,128)(2,1)}, bf16[32,12288]{1,0:T(8,128)(2,1)}, u32[]{:S(2)}, u32[]{:S(2)}) collective-permute-start(bf16[32,12288]{1,0:T(8,128)(2,1)} %get-tuple-element.854), channel_id=1, source_target_pairs={{8,0},{16,8},{24,16},{9,1},{17,9},{25,17},{10,2},{18,10},{26,18},{... | collective-permute-start | bytes 2359304 | tf_op jit(solution)/shard_map/while/body/eval_jaxpr/ppermute | solution.py:25
  378.4 4.9 copy-start.4
  380.0 5.9 slice-start
  383.2 2.7 slice-start.1
  384.6 3.4 slice-start.2
  393.2 13.6 %collective-permute-start.1 = (bf16[32,12288]{1,0:T(8,128)(2,1)}, bf16[32,12288]{1,0:T(8,128)(2,1)}, u32[]{:S(2)}, u32[]{:S(2)}) collective-permute-start(bf16[32,12288]{1,0:T(8,128)(2,1)} %get-tuple-element.854), channel_id=1, source_target_pairs={{8,0},{16,8},{24,16},{9,1},{17,9},{25,17},{10,2},{18,10},{26,18},{... | collective-permute-start | bytes 2359304 | tf_op jit(solution)/shard_map/while/body/eval_jaxpr/ppermute | solution.py:25
  406.9 4.9 copy-start.4
  408.5 5.9 slice-start
  411.7 2.7 slice-start.1
  413.1 3.4 slice-start.2
  421.7 13.6 %collective-permute-start.1 = (bf16[32,12288]{1,0:T(8,128)(2,1)}, bf16[32,12288]{1,0:T(8,128)(2,1)}, u32[]{:S(2)}, u32[]{:S(2)}) collective-permute-start(bf16[32,12288]{1,0:T(8,128)(2,1)} %get-tuple-element.854), channel_id=1, source_target_pairs={{8,0},{16,8},{24,16},{9,1},{17,9},{25,17},{10,2},{18,10},{26,18},{... | collective-permute-start | bytes 2359304 | tf_op jit(solution)/shard_map/while/body/eval_jaxpr/ppermute | solution.py:25
  435.4 4.9 copy-start.4
  437.0 5.9 slice-start
  441.6 3.4 slice-start.2
  450.2 4.5 collective-permute-start.1
  454.8 240.8 %reduce-scatter.5.cloned.1.call-start = ((), (), s32[]{:S(2)}) async-start(), calls=%async_computation.5 | async-start | bytes 7077888 | tf_op jit(solution)/shard_map/reduce_scatter | solution.py:206
  454.8 284.1 %copy-start.6 = (f32[1,128,1536]{2,1,0:T(8,128)S(1)}, f32[1,128,1536]{2,1,0:T(8,128)}, u32[]{:S(2)}) copy-start(f32[1,128,1536]{2,1,0:T(8,128)} %param.21) | copy-start | bytes 2359300
  454.8 284.1 %copy-start.9 = (f32[1,128,1536]{2,1,0:T(8,128)S(1)}, f32[1,128,1536]{2,1,0:T(8,128)}, u32[]{:S(2)}) copy-start(f32[1,128,1536]{2,1,0:T(8,128)} %param.25) | copy-start | bytes 2359300
  576.9 165.5 %copy-start.7 = (f32[1,1536,128]{2,1,0:T(8,128)S(1)}, f32[1,1536,128]{2,1,0:T(8,128)}, u32[]{:S(2)}) copy-start(f32[1,1536,128]{2,1,0:T(8,128)} %param.20) | copy-start | bytes 2359300
  576.9 165.5 %copy-start.8 = (f32[1536,128]{1,0:T(8,128)S(1)}, f32[1536,128]{1,0:T(8,128)}, u32[]{:S(2)}) copy-start(f32[1536,128]{1,0:T(8,128)} %reduce-scatter.3.cloned.1.call-done) | copy-start | bytes 2359300
  738.9 3.5 copy-start.10
  739.0 3.5 copy-start.11
  (13 other events, 31.9 us)
Sparse Core Ops, SparseCore 0:
  10.8 63.1 all-gather.2
  76.7 59.1 all-gather.4
  454.9 120.0 reduce-scatter.2
  578.4 117.0 reduce-scatter.4
where the time goes:
time: 753 us; the launch traced here: 751 us
  waiting for transfers between devices  466 us (62%)
  starting transfers between devices  73.3 us (10%)
  other arithmetic  57.4 us (8%)
  local copies, waits for them, and re-layouts  52.2 us (7%)
  matrix products  45.8 us (6%)
  blocking collectives  39.4 us (5%)
  between operations  15.9 us (2%)
    reduce_scatter x1, waiting for transfers between devices, shards(): lax.psum_scatter(full_in, 'dp', scatter_dimension=0, tiled=True)  120 us
    reduce_scatter x1, waiting for transfers between devices, shards(): lax.psum_scatter(full_out, 'dp', scatter_dimension=1, tiled=True)  119 us
    ppermute x14, waiting for transfers between devices, passed_along(): return lax.ppermute(block, axis, route)  103 us
    ppermute x14, starting transfers between devices, passed_along(): return lax.ppermute(block, axis, route)  73.1 us
    all_gather x1, waiting for transfers between devices, shards(): lax.all_gather(master_in[0].astype(jnp.bfloat16), 'dp', axis=0, tiled=True)  62.7 us
    all_gather x1, waiting for transfers between devices, shards(): lax.all_gather(master_out[0].astype(jnp.bfloat16), 'dp', axis=1, tiled=True)  61.9 us
    psum x1, blocking collectives, shards(): total_sq = lax.psum(local_sq, ('section', 'dp'))  39.4 us
    dynamic_update_slice x21, other arithmetic, store_block(): lax.dynamic_update_index_in_dim(buffer, jnp.where(in_range, values, old_b...  31.3 us
  transfers between devices with their start and end apart: 18, of which 11 were waited for; matrix products, arithmetic and copies ran while one was open for 4% of the time, Pallas kernels for 0%

commit v1 on v0

v1 whole, which is shorter than its diff:
```python
import functools
import math

import jax
import jax.numpy as jnp
from jax import lax
from jax.experimental import pallas as pl
from jax.experimental.pallas import tpu as pltpu
from jax.sharding import PartitionSpec as P

STEP = 10

norm_eps = 1e-05
gelu_coef = 0.7978845608028654
beta_one = 0.9
beta_two = 0.95
adam_eps = 1e-08
learn_rate = 0.05
decay_rate = 0.1
clip_rms = 0.5

BF16 = jnp.bfloat16
F32 = jnp.float32


def gelu_pair(hidden_pre):
    inner_arg = gelu_coef * (hidden_pre + 0.044715 * hidden_pre * hidden_pre * hidden_pre)
    tangent = jnp.tanh(inner_arg)
    gelu_value = 0.5 * hidden_pre * (1.0 + tangent)
    gelu_slope = 0.5 * (1.0 + tangent) + 0.5 * hidden_pre * (
        1.0 - tangent * tangent
    ) * gelu_coef * (1.0 + 3.0 * 0.044715 * hidden_pre * hidden_pre)
    return (gelu_value, gelu_slope)


def contract_rows(left_arr, right_arr):
    return lax.dot_general(
        left_arr, right_arr, (((0,), (0,)), ((), ())), preferred_element_type=F32
    )


def contract_last(left_arr, right_arr):
    return lax.dot_general(
        left_arr, right_arr, (((1,), (1,)), ((), ())), preferred_element_type=F32
    )


def adam_update(master, first, second, grad):
    first_new = beta_one * first + (1.0 - beta_one) * grad
    second_new = beta_two * second + (1.0 - beta_two) * grad * grad
    first_hat = first_new / (1.0 - beta_one**STEP)
    second_hat = second_new / (1.0 - beta_two**STEP)
    master_new = master - learn_rate * (
        first_hat / (jnp.sqrt(second_hat) + adam_eps) + decay_rate * master
    )
    return (master_new, first_new, second_new)


def split_halves(column, width):
    high = column.astype(BF16)
    low = (column - high.astype(F32)).astype(BF16)
    shape = (column.shape[0], width)
    return jnp.concatenate(
        [jnp.broadcast_to(high, shape), jnp.broadcast_to(low, shape)], axis=1
    )


def join_halves(values, rank):
    half = rank + rank // 2
    return values[:, rank : rank + 1].astype(F32) + values[:, half : half + 1].astype(F32)


def stack_kernel(
    S, DP, rb, F, R, D,
    x_hbm, cot_hbm, gain_hbm, win_hbm, wout_hbm,
    out_hbm, gin_ref, gout_ref, tot_ref,
    xs, cot, delta, gains, wi, wo,
    pay_f, rs_f, ag_f, pay_b, rs_b, ag_b,
    pre_keep, sum_keep, inv_keep,
    gi_send, go_send, gi_recv, go_recv, sq_send, sq_recv,
    x_send, x_recv, c_send, c_recv, gn_send, gn_recv,
    wi_ssem, wi_rsem, wo_ssem, wo_rsem,
    pf_s, pf_r, af_s, af_r, pb_s, pb_r, ab_s, ab_r,
    o_send, o_recv, g_send, g_recv, h_send, h_recv, q_send, q_recv,
):
    q = lax.axis_index("section")
    d = lax.axis_index("dp")
    N = S * DP
    T = DP * rb

    def place(sec, dp):
        return {"section": sec, "dp": dp}

    def send(src, dst, ssem, rsem, sec, dp):
        pltpu.make_async_remote_copy(
            src_ref=src, dst_ref=dst, send_sem=ssem, recv_sem=rsem,
            device_id=place(sec, dp), device_id_type=pl.DeviceIdType.MESH,
        ).start()

    def wait_bytes(ref, sem):
        pltpu.make_async_copy(ref, ref, sem).wait()

    def rows(block):
        return pl.ds(pl.multiple_of(block * rb, rb), rb)

    def cols(block):
        return pl.ds(pl.multiple_of(block * F, 128), F)

    me = q * DP + d
    barrier = pltpu.get_barrier_semaphore()

    def greet(j, carry):
        other = lax.rem(me + j, N)
        pl.semaphore_signal(
            barrier, inc=1, device_id=place(other // DP, lax.rem(other, DP)),
            device_id_type=pl.DeviceIdType.MESH,
        )
        return carry

    lax.fori_loop(1, N, greet, 0)
    pl.semaphore_wait(barrier, N - 1)

    def spread_rows(src_hbm, dst, ssem, rsem):
        def body(i, carry):
            peer = lax.rem(d + i, DP)
            send(src_hbm.at[rows(q), cols(peer)], dst.at[rows(d), :], ssem, rsem, q, peer)
            return carry

        lax.fori_loop(1, DP, body, 0)
        pltpu.make_async_copy(src_hbm.at[rows(q), cols(d)], dst.at[rows(d), :], rsem).start()

    def spread_layers(src, dst, ssem, rsem):
        for j in [S // 2] + [k for k in range(1, S) if k != S // 2]:
            send(src, dst.at[q], ssem, rsem.at[q], lax.rem(q + j, S), d)
        pltpu.make_async_copy(src, dst.at[q], rsem.at[q]).start()

    def exchange(src_of, dst, ssem, rsem):
        def body(i, carry):
            peer = lax.rem(d + i, DP)
            send(src_of(peer), dst.at[rows(d), :], ssem, rsem, q, peer)
            return carry

        lax.fori_loop(1, DP, body, 0)

    head = pl.ds(0, (DP - 1) * rb)

    spread_layers(gain_hbm.at[:, cols(d)], gains, gn_send, gn_recv)
    spread_rows(x_hbm, xs.at[pl.ds(0, T)], x_send, x_recv)
    spread_layers(win_hbm, wi, wi_ssem, wi_rsem)
    wait_bytes(xs.at[pl.ds(0, T)], x_recv)
    spread_layers(wout_hbm, wo, wo_ssem, wo_rsem)
    spread_rows(cot_hbm, cot, c_send, c_recv)

    def layer_rows(l):
        return pl.ds(l * T, T)

    def send_outputs(l):
        base = (l + 1) * T

        def block(peer):
            return xs.at[pl.ds(pl.multiple_of(base + peer * rb, rb), rb), :]

        def body(i, carry):
            peer = lax.rem(d + i, DP)
            send(block(peer), out_hbm.at[rows(q), cols(d)], o_send, o_recv, l, peer)
            return carry

        lax.fori_loop(1, DP, body, 0)

        @pl.when(q != l)
        def _():
            send(block(d), out_hbm.at[rows(q), cols(d)], o_send, o_recv, l, d)

        @pl.when(q == l)
        def _():
            pltpu.make_async_copy(block(d), out_hbm.at[rows(q), cols(d)], o_recv).start()

    for l in range(S):
        wait_bytes(gains.at[l], gn_recv.at[l])
        wait_bytes(wi.at[l], wi_rsem.at[l])
        wide = xs[layer_rows(l), :].astype(F32)
        part = jnp.dot((wide * gains[l]).astype(BF16), wi[l], preferred_element_type=F32)
        squares = jnp.sum(wide * wide, axis=1, keepdims=True)
        pay_f[l] = jnp.concatenate([part.astype(BF16), split_halves(squares, R // 2)], axis=1)
        exchange(lambda peer: pay_f.at[l, rows(peer), :], rs_f.at[l], pf_s.at[l], pf_r.at[l])
        rs_f[l, rows(d), :] = pay_f[l, rows(d), :]
        if l > 0:
            send_outputs(l - 1)
        wait_bytes(rs_f.at[l, head], pf_r.at[l])
        total = rs_f[l, 0:rb, :].astype(F32)
        for b in range(1, DP):
            total = total + rs_f[l, b * rb : (b + 1) * rb, :].astype(F32)
        inv = lax.rsqrt(join_halves(total, R) / D + norm_eps)
        pre = total[:, :R] * inv
        act, _ = gelu_pair(pre)
        pre_keep[l] = pre
        sum_keep[l] = total[:, :R]
        inv_keep[l] = jnp.broadcast_to(inv, (rb, R))
        ag_f[l, rows(d), :] = jnp.concatenate(
            [act.astype(BF16), split_halves(inv, R // 2)], axis=1
        )
        exchange(lambda peer: ag_f.at[l, rows(d), :], ag_f.at[l], af_s.at[l], af_r.at[l])
        wait_bytes(wo.at[l], wo_rsem.at[l])
        wait_bytes(ag_f.at[l, head], af_r.at[l])
        xs[layer_rows(l + 1), :] = (
            xs[layer_rows(l), :].astype(F32)
            + jnp.dot(ag_f[l, :, :R], wo[l], preferred_element_type=F32)
        ).astype(BF16)

    wait_bytes(cot, c_recv)

    def send_grads(l, incoming):
        normed = (
            xs[layer_rows(l), :].astype(F32) * join_halves(ag_f[l], R) * gains[l]
        ).astype(BF16)
        grad_in = contract_rows(normed, ag_b[l, :, :R])
        grad_out = contract_rows(ag_f[l, :, :R], incoming[...])

        @pl.when(q == l)
        def _():
            gin_ref[...] = grad_in
            gout_ref[...] = grad_out

        @pl.when(q != l)
        def _():
            gi_send[l] = grad_in.astype(BF16)
            go_send[l] = grad_out.astype(BF16)
            slot = lax.rem(q - l - 1 + 2 * S, S)
            send(gi_send.at[l], gi_recv.at[slot], g_send, g_recv, l, d)
            send(go_send.at[l], go_recv.at[slot], h_send, h_recv, l, d)

    for step in range(S):
        l = S - 1 - step
        incoming = cot if step == 0 else delta.at[step - 1]
        part = contract_last(incoming[...], wo[l])
        pay_b[l] = part.astype(BF16)
        exchange(lambda peer: pay_b.at[l, rows(peer), :], rs_b.at[l], pb_s.at[l], pb_r.at[l])
        rs_b[l, rows(d), :] = pay_b[l, rows(d), :]
        if step == 0:
            send_outputs(S - 1)
        else:
            send_grads(l + 1, cot if step == 1 else delta.at[step - 2])
        wait_bytes(rs_b.at[l, head], pb_r.at[l])
        total = rs_b[l, 0:rb, :].astype(F32)
        for b in range(1, DP):
            total = total + rs_b[l, b * rb : (b + 1) * rb, :].astype(F32)
        _, slope = gelu_pair(pre_keep[l])
        d_pre = (total * slope).astype(BF16)
        inv = inv_keep[l][:, 0:1]
        mean = jnp.sum(d_pre.astype(F32) * sum_keep[l], axis=1, keepdims=True) / D
        ag_b[l, rows(d), :] = jnp.concatenate(
            [d_pre, split_halves(inv * inv * inv * mean, R // 2)], axis=1
        )
        exchange(lambda peer: ag_b.at[l, rows(d), :], ag_b.at[l], ab_s.at[l], ab_r.at[l])
        wait_bytes(ag_b.at[l, head], ab_r.at[l])

        if l > 0:
            scaled = contract_last(ag_b[l, :, :R], wi[l]) * gains[l]
            delta[step] = (
                incoming[...].astype(F32)
                + join_halves(ag_f[l], R) * scaled
                - xs[layer_rows(l), :].astype(F32) * join_halves(ag_b[l], R)
            ).astype(BF16)

        if l == 0:
            send_grads(0, incoming)

    wait_bytes(gi_recv, g_recv)
    wait_bytes(go_recv, h_recv)
    grad_in = gin_ref[...]
    grad_out = gout_ref[...]
    for k in range(S - 1):
        grad_in = grad_in + gi_recv[k].astype(F32)
        grad_out = grad_out + go_recv[k].astype(F32)
    gin_ref[...] = grad_in
    gout_ref[...] = grad_out
    sq = jnp.sum((grad_in * grad_in).reshape(F // 8, 8, R), axis=0)
    sq_out = jnp.sum((grad_out * grad_out).reshape(R // 8, 8, F), axis=0)
    for k in range(F // 128):
        sq = sq + sq_out[:, k * 128 : (k + 1) * 128]
    sq_send[...] = sq

    def tell(j, carry):
        other = lax.rem(me + j, N)
        send(
            sq_send, sq_recv.at[pl.ds(pl.multiple_of((N - 1 - j) * 8, 8), 8), :],
            q_send, q_recv, other // DP, lax.rem(other, DP),
        )
        return carry

    lax.fori_loop(1, N, tell, 0)
    wait_bytes(sq_recv, q_recv)
    tot_ref[...] = sq + jnp.sum(sq_recv[...].reshape(N - 1, 8, 128), axis=0)

    wait_bytes(out_hbm, o_recv)
    wait_bytes(xs.at[pl.ds(0, (N - 1) * rb)], o_send)
    wait_bytes(xs.at[head], x_send)
    wait_bytes(xs.at[head], c_send)
    wait_bytes(gains.at[pl.ds(0, S - 1)], gn_send)
    wait_bytes(wi.at[pl.ds(0, S - 1)], wi_ssem)
    wait_bytes(wo.at[pl.ds(0, S - 1)], wo_ssem)
    wait_bytes(gi_recv, g_send)
    wait_bytes(go_recv, h_send)
    wait_bytes(sq_recv, q_send)
    for l in range(S):
        wait_bytes(rs_f.at[l, head], pf_s.at[l])
        wait_bytes(ag_f.at[l, head], af_s.at[l])
        wait_bytes(rs_b.at[l, head], pb_s.at[l])
        wait_bytes(ag_b.at[l, head], ab_s.at[l])


def run_stack(x, cot, gain, win, wout):
    S = lax.axis_size("section")
    DP = lax.axis_size("dp")
    tok, D = x.shape
    F, R = win.shape
    rb = tok // S
    T = DP * rb
    N = S * DP
    sem = pltpu.SemaphoreType.DMA
    any_spec = pl.BlockSpec(memory_space=pl.ANY)
    vmem_spec = pl.BlockSpec(memory_space=pltpu.VMEM)
    scratch = [
        pltpu.VMEM(((S + 1) * T, F), BF16),
        pltpu.VMEM((T, F), BF16),
        pltpu.VMEM((S, T, F), BF16),
        pltpu.VMEM((S, 1, F), F32),
        pltpu.VMEM((S, F, R), BF16),
        pltpu.VMEM((S, R, F), BF16),
        pltpu.VMEM((S, T, 2 * R), BF16),
        pltpu.VMEM((S, T, 2 * R), BF16),
        pltpu.VMEM((S, T, 2 * R), BF16),
        pltpu.VMEM((S, T, R), BF16),
        pltpu.VMEM((S, T, R), BF16),
        pltpu.VMEM((S, T, 2 * R), BF16),
        pltpu.VMEM((S, rb, R), F32),
        pltpu.VMEM((S, rb, R), F32),
        pltpu.VMEM((S, rb, R), F32),
        pltpu.VMEM((S, F, R), BF16),
        pltpu.VMEM((S, R, F), BF16),
        pltpu.VMEM((S - 1, F, R), BF16),
        pltpu.VMEM((S - 1, R, F), BF16),
        pltpu.VMEM((8, 128), F32),
        pltpu.VMEM(((N - 1) * 8, 128), F32),
        sem, sem, sem, sem, sem, sem((S,)),
        sem, sem((S,)), sem, sem((S,)),
        sem((S,)), sem((S,)), sem((S,)), sem((S,)),
        sem((S,)), sem((S,)), sem((S,)), sem((S,)),
        sem, sem, sem, sem, sem, sem, sem, sem,
    ]
    return pl.pallas_call(
        functools.partial(stack_kernel, S, DP, rb, F, R, D),
        out_shape=(
            jax.ShapeDtypeStruct((tok, D), BF16),
            jax.ShapeDtypeStruct((F, R), F32),
            jax.ShapeDtypeStruct((R, F), F32),
            jax.ShapeDtypeStruct((8, 128), F32),
        ),
        in_specs=[any_spec] * 5,
        out_specs=(any_spec, vmem_spec, vmem_spec, vmem_spec),
        scratch_shapes=scratch,
        compiler_params=pltpu.CompilerParams(
            collective_id=0, has_side_effects=True, vmem_limit_bytes=56 * 1024 * 1024
        ),
        name="adapter_stack",
    )(x, cot, gain, win, wout)


def shards(
    stack_input, out_cotangent, norm_gain, master_in, master_out,
    first_in, first_out, second_in, second_out,
):
    num_sections = lax.axis_size("section")
    model_width = stack_input.shape[1]
    rank_width = master_in.shape[2]
    section_rows, shard_in, shard_out, squares = run_stack(
        stack_input, out_cotangent, norm_gain,
        master_in[0].astype(BF16), master_out[0].astype(BF16),
    )
    total_sq = jnp.sum(squares)
    norm_limit = clip_rms * math.sqrt(2.0 * model_width * rank_width * num_sections)
    clip_factor = norm_limit / jnp.maximum(jnp.sqrt(total_sq), norm_limit)
    new_in, new_first_in, new_second_in = adam_update(
        master_in[0], first_in[0], second_in[0], clip_factor * shard_in
    )
    new_out, new_first_out, new_second_out = adam_update(
        master_out[0], first_out[0], second_out[0], clip_factor * shard_out
    )
    return (
        section_rows[None],
        new_in[None],
        new_out[None],
        new_first_in[None],
        new_first_out[None],
        new_second_in[None],
        new_second_out[None],
    )


def solution(mesh):
    in_specs = (
        P("dp", None),
        P("dp", None),
        P("section", None),
        P("section", "dp", None),
        P("section", None, "dp"),
        P("section", "dp", None),
        P("section", None, "dp"),
        P("section", "dp", None),
        P("section", None, "dp"),
    )
    out_specs = (
        P("section", "dp", None),
        P("section", "dp", None),
        P("section", None, "dp"),
        P("section", "dp", None),
        P("section", None, "dp"),
        P("section", "dp", None),
        P("section", None, "dp"),
    )
    return jax.shard_map(shards, mesh=mesh, in_specs=in_specs, out_specs=out_specs, check_vma=False)
```

time: 753 us -> 224 us (0.30)
  waiting for transfers between devices: 466 us -> 0 us
  Pallas kernels: 0 us -> 209 us
  starting transfers between devices: 73.3 us -> 0 us
  local copies, waits for them, and re-layouts: 52.2 us -> 2.25 us
  other arithmetic: 57.4 us -> 10.5 us
  matrix products: 45.8 us -> 0 us
  blocking collectives: 39.4 us -> 0 us
  between operations: 15.9 us -> 1.45 us
    reduce_scatter x2 -> x0, waiting for transfers between devices: 238 us -> none  [the longest x1 120 us: shards(): lax.psum_scatter(full_in, 'dp', scatter_dimension=0, tiled=True)]
    pallas_call x0 -> x1, Pallas kernels: none -> 209 us  [run_stack(): pl.pallas_call(functools.partial(stack_kernel, S, DP, rb, F, R, D), out_s...]
    all_gather x2 -> x0, waiting for transfers between devices: 125 us -> none  [the longest x1 62.7 us: shards(): lax.all_gather(master_in[0].astype(jnp.bfloat16), 'dp', axis=0, tiled=True)]
    ppermute x14 -> x0, waiting for transfers between devices: 103 us -> none  [passed_along(): return lax.ppermute(block, axis, route)]
    ppermute x14 -> x0, starting transfers between devices: 73.1 us -> none  [passed_along(): return lax.ppermute(block, axis, route)]
    dot_general x24 -> x0, matrix products: 45.8 us -> none  [the longest x8 18.2 us: contract_last(): lax.dot_general(left_arr, right_arr, (((1,), (1,)), ((), ())), preferred_...]
    psum x1 -> x0, blocking collectives: 39.4 us -> none  [shards(): total_sq = lax.psum(local_sq, ('section', 'dp'))]
    dynamic_update_slice x21 -> x0, other arithmetic: 31.3 us -> none  [store_block(): lax.dynamic_update_index_in_dim(buffer, jnp.where(in_range, values, old_b...]
  transfers between devices with their start and end apart: 18 -> 0, of which waited for: 11 -> 0; matrix products, arithmetic and copies ran while one was open for 4% -> 0% of each run, Pallas kernels for 0% -> 0%
where the time goes in v1:
time: 224 us; the launch traced here: 223 us
  Pallas kernels  209 us (93%)
  other arithmetic  10.5 us (5%)
  local copies, waits for them, and re-layouts  2.25 us (1%)
    pallas_call x1, Pallas kernels, run_stack(): pl.pallas_call(functools.partial(stack_kernel, S, DP, rb, F, R, D), out_s...  209 us

profile of v1, /device:TPU:0, one launch (start us, length us, event | category | flops | bytes accessed | tf_op | source)
XLA Modules:
  0.0 223.4 jit_solution(15369980161620377233)
XLA Ops:
  0.6 1.9 bitcast_convert_fusion.1.win_hbm
  2.6 1.9 bitcast_convert_fusion.wout_hbm
  4.5 0.0 copy-start.1
  4.5 0.0 copy-start.3
  4.5 0.0 copy-start.4
  4.5 209.2 %adapter_stack.1 = (bf16[128,12288]{1,0:T(8,128)(2,1)}, f32[1536,128]{1,0:T(8,128)}, f32[128,1536]{1,0:T(8,128)}, f32[8,128]{1,0:T(8,128)}) custom-call(bf16[128,12288]{1,0:T(8,128)(2,1)} %x_hbm.1, bf16[128,12288]{1,0:T(8,128)(2,1)} %cot_hbm.1, f32[1,12288]{1,0:T(1,128)} %gain_hbm.1, bf16[1536,128]{1,0:T(8,128)(2,1)} %bitcast_convert_fusion.1.win_hbm, ...), custom_call_target="tpu_custom_call" | custom-call | tf_op jit(solution)/shard_map/adapter_stack/pallas_call | solution.py:351
  213.7 0.0 copy-start.2
  213.7 1.4 reduce_sum.9
  215.8 0.0 copy-start.5
  215.8 0.0 copy-start.6
  215.8 0.0 copy-start.7
  215.8 0.0 copy-done.1
  215.8 0.0 copy-done.3
  215.8 0.0 copy-done.4
  215.9 3.3 %fusion.10 = (f32[1,128,1536]{2,1,0:T(8,128)}, f32[1,128,1536]{2,1,0:T(8,128)}, f32[1,128,1536]{2,1,0:T(8,128)}) fusion(f32[128,1536]{1,0:T(8,128)} %get-tuple-element.14, f32[]{:T(128)S(6)} %div.33, f32[1,128,1536]{2,1,0:T(8,128)S(1)} %copy-done.3, f32[1,128,1536]{2,1,0:T(8,128)S(1)} %copy-done.4, f32[1,128,1536]{2,1,0:T(8,128)S(1)} %copy-done.1), kind=kLoop, calls=%fused_computation.20 | loop fusion | flops 3145728 | bytes 5505028 | tf_op jit(solution)/shard_map/broadcast_in_dim | solution.py:396
  219.2 0.0 copy-start
  219.2 0.0 copy-done.2
  219.2 0.0 copy-done.5
  219.2 0.0 copy-done.6
  219.2 0.0 copy-done.7
  219.2 2.0 fusion.11
  221.2 0.6 copy-done
  221.8 1.7 copy.17
Async XLA Ops:
  4.5 211.4 %copy-start.1 = (f32[1,128,1536]{2,1,0:T(8,128)S(1)}, f32[1,128,1536]{2,1,0:T(8,128)}, u32[]{:S(2)}) copy-start(f32[1,128,1536]{2,1,0:T(8,128)} %param.13) | copy-start | bytes 2359300
  4.5 211.4 %copy-start.3 = (f32[1,128,1536]{2,1,0:T(8,128)S(1)}, f32[1,128,1536]{2,1,0:T(8,128)}, u32[]{:S(2)}) copy-start(f32[1,128,1536]{2,1,0:T(8,128)} %param.17) | copy-start | bytes 2359300
  4.5 211.4 %copy-start.4 = (f32[1,128,1536]{2,1,0:T(8,128)S(1)}, f32[1,128,1536]{2,1,0:T(8,128)}, u32[]{:S(2)}) copy-start(f32[1,128,1536]{2,1,0:T(8,128)} %param.15) | copy-start | bytes 2359300
  213.7 5.5 %copy-start.2 = (f32[1,1536,128]{2,1,0:T(8,128)S(1)}, f32[1,1536,128]{2,1,0:T(8,128)}, u32[]{:S(2)}) copy-start(f32[1,1536,128]{2,1,0:T(8,128)} %param.12) | copy-start | bytes 2359300
  215.8 3.4 %copy-start.5 = (f32[1,1536,128]{2,1,0:T(8,128)S(1)}, f32[1,1536,128]{2,1,0:T(8,128)}, u32[]{:S(2)}) copy-start(f32[1,1536,128]{2,1,0:T(8,128)} %param.16) | copy-start | bytes 2359300
  215.8 3.4 %copy-start.6 = (f32[1,1536,128]{2,1,0:T(8,128)S(1)}, f32[1,1536,128]{2,1,0:T(8,128)}, u32[]{:S(2)}) copy-start(f32[1,1536,128]{2,1,0:T(8,128)} %param.14) | copy-start | bytes 2359300
  215.8 3.4 %copy-start.7 = (f32[1536,128]{1,0:T(8,128)S(1)}, f32[1536,128]{1,0:T(8,128)}, u32[]{:S(2)}) copy-start(f32[1536,128]{1,0:T(8,128)} %get-tuple-element.13) | copy-start | bytes 2359300
  219.2 2.6 %copy-start = (bf16[128,12288]{1,0:T(8,128)(2,1)S(1)}, bf16[128,12288]{1,0:T(8,128)(2,1)}, u32[]{:S(2)}) copy-start(bf16[128,12288]{1,0:T(8,128)(2,1)} %get-tuple-element.11) | copy-start | bytes 9437188

commit v2 on v1

--- a/solution.py
+++ b/solution.py
@@ -65,14 +65,14 @@
     )
 
 
-def join_halves(values, rank):
-    half = rank + rank // 2
-    return values[:, rank : rank + 1].astype(F32) + values[:, half : half + 1].astype(F32)
+def join_halves(values, start, width):
+    high = values[:, start : start + 1].astype(F32)
+    return high + values[:, start + width : start + width + 1].astype(F32)
 
 
 def stack_kernel(
     S, DP, rb, F, R, D,
-    x_hbm, cot_hbm, gain_hbm, win_hbm, wout_hbm,
+    x_hbm, cot_hbm, gain_hbm, win_ref, wout_ref,
     out_hbm, gin_ref, gout_ref, tot_ref,
     xs, cot, delta, gains, wi, wo,
     pay_f, rs_f, ag_f, pay_b, rs_b, ag_b,
@@ -118,21 +118,28 @@
         return carry
 
     lax.fori_loop(1, N, greet, 0)
+    own_gain = pltpu.make_async_copy(gain_hbm.at[:, cols(d)], gains.at[q], gn_recv.at[q])
+    own_gain.start()
+    wi[q] = win_ref[...].astype(BF16)
+    wo[q] = wout_ref[...].astype(BF16)
+    own_gain.wait()
     pl.semaphore_wait(barrier, N - 1)
 
-    def spread_rows(src_hbm, dst, ssem, rsem):
-        def body(i, carry):
+    def send_rows(i, src_hbm, dst, ssem, rsem):
+        if i == 0:
+            pltpu.make_async_copy(src_hbm.at[rows(q), cols(d)], dst.at[rows(d), :], rsem).start()
+        else:
             peer = lax.rem(d + i, DP)
             send(src_hbm.at[rows(q), cols(peer)], dst.at[rows(d), :], ssem, rsem, q, peer)
-            return carry
-
-        lax.fori_loop(1, DP, body, 0)
-        pltpu.make_async_copy(src_hbm.at[rows(q), cols(d)], dst.at[rows(d), :], rsem).start()
 
     def spread_layers(src, dst, ssem, rsem):
         for j in [S // 2] + [k for k in range(1, S) if k != S // 2]:
             send(src, dst.at[q], ssem, rsem.at[q], lax.rem(q + j, S), d)
-        pltpu.make_async_copy(src, dst.at[q], rsem.at[q]).start()
+
+    def wait_layer(buffer, rsem, l):
+        @pl.when(q != l)
+        def _():
+            wait_bytes(buffer.at[l], rsem.at[l])
 
     def exchange(src_of, dst, ssem, rsem):
         def body(i, carry):
@@ -144,90 +151,103 @@
 
     head = pl.ds(0, (DP - 1) * rb)
 
-    spread_layers(gain_hbm.at[:, cols(d)], gains, gn_send, gn_recv)
-    spread_rows(x_hbm, xs.at[pl.ds(0, T)], x_send, x_recv)
-    spread_layers(win_hbm, wi, wi_ssem, wi_rsem)
+    for i in range(DP):
+        send_rows(i, x_hbm, xs.at[pl.ds(0, T)], x_send, x_recv)
+    spread_layers(gains.at[q], gains, gn_send, gn_recv)
+    spread_layers(wi.at[q], wi, wi_ssem, wi_rsem)
     wait_bytes(xs.at[pl.ds(0, T)], x_recv)
-    spread_layers(wout_hbm, wo, wo_ssem, wo_rsem)
-    spread_rows(cot_hbm, cot, c_send, c_recv)
+    spread_layers(wo.at[q], wo, wo_ssem, wo_rsem)
 
     def layer_rows(l):
         return pl.ds(l * T, T)
 
-    def send_outputs(l):
-        base = (l + 1) * T
-
-        def block(peer):
-            return xs.at[pl.ds(pl.multiple_of(base + peer * rb, rb), rb), :]
-
-        def body(i, carry):
-            peer = lax.rem(d + i, DP)
-            send(block(peer), out_hbm.at[rows(q), cols(d)], o_send, o_recv, l, peer)
-            return carry
-
-        lax.fori_loop(1, DP, body, 0)
+    def send_output(l, i):
+        peer = lax.rem(d + i, DP)
+        block = xs.at[pl.ds(pl.multiple_of((l + 1) * T + peer * rb, rb), rb), :]
+        target = out_hbm.at[rows(q), cols(d)]
+        if i > 0:
+            send(block, target, o_send, o_recv, l, peer)
+            return
 
         @pl.when(q != l)
         def _():
-            send(block(d), out_hbm.at[rows(q), cols(d)], o_send, o_recv, l, d)
+            send(block, target, o_send, o_recv, l, peer)
 
         @pl.when(q == l)
         def _():
-            pltpu.make_async_copy(block(d), out_hbm.at[rows(q), cols(d)], o_recv).start()
+            pltpu.make_async_copy(block, target, o_recv).start()
+
+    waiting_cot = list(range(DP))
+    waiting_out = []
+
+    def send_some_cot(count):
+        for _ in range(min(count, len(waiting_cot))):
+            send_rows(waiting_cot.pop(0), cot_hbm, cot, c_send, c_recv)
+
+    def send_some_out(count):
+        for _ in range(min(count, len(waiting_out))):
+            send_output(*waiting_out.pop(0))
+
+    def send_bulk():
+        if waiting_cot:
+            send_some_cot(-(-DP // 4))
+        else:
+            send_some_out(-(-DP * S // (3 * S - 1)))
 
     for l in range(S):
-        wait_bytes(gains.at[l], gn_recv.at[l])
-        wait_bytes(wi.at[l], wi_rsem.at[l])
+        wait_layer(gains, gn_recv, l)
+        wait_layer(wi, wi_rsem, l)
         wide = xs[layer_rows(l), :].astype(F32)
         part = jnp.dot((wide * gains[l]).astype(BF16), wi[l], preferred_element_type=F32)
         squares = jnp.sum(wide * wide, axis=1, keepdims=True)
         pay_f[l] = jnp.concatenate([part.astype(BF16), split_halves(squares, R // 2)], axis=1)
         exchange(lambda peer: pay_f.at[l, rows(peer), :], rs_f.at[l], pf_s.at[l], pf_r.at[l])
         rs_f[l, rows(d), :] = pay_f[l, rows(d), :]
-        if l > 0:
-            send_outputs(l - 1)
+        send_bulk()
         wait_bytes(rs_f.at[l, head], pf_r.at[l])
         total = rs_f[l, 0:rb, :].astype(F32)
         for b in range(1, DP):
             total = total + rs_f[l, b * rb : (b + 1) * rb, :].astype(F32)
-        inv = lax.rsqrt(join_halves(total, R) / D + norm_eps)
+        inv = lax.rsqrt(join_halves(total, R, R // 2) / D + norm_eps)
         pre = total[:, :R] * inv
         act, _ = gelu_pair(pre)
         pre_keep[l] = pre
         sum_keep[l] = total[:, :R]
         inv_keep[l] = jnp.broadcast_to(inv, (rb, R))
-        ag_f[l, rows(d), :] = jnp.concatenate(
-            [act.astype(BF16), split_halves(inv, R // 2)], axis=1
-        )
+        ag_f[l, rows(d), :] = act.astype(BF16)
         exchange(lambda peer: ag_f.at[l, rows(d), :], ag_f.at[l], af_s.at[l], af_r.at[l])
-        wait_bytes(wo.at[l], wo_rsem.at[l])
+        send_bulk()
+        wait_layer(wo, wo_rsem, l)
         wait_bytes(ag_f.at[l, head], af_r.at[l])
         xs[layer_rows(l + 1), :] = (
             xs[layer_rows(l), :].astype(F32)
-            + jnp.dot(ag_f[l, :, :R], wo[l], preferred_element_type=F32)
+            + jnp.dot(ag_f[l], wo[l], preferred_element_type=F32)
         ).astype(BF16)
-
+        waiting_out.extend((l, i) for i in range(DP))
+
+    send_some_cot(DP)
     wait_bytes(cot, c_recv)
 
-    def send_grads(l, incoming):
-        normed = (
-            xs[layer_rows(l), :].astype(F32) * join_halves(ag_f[l], R) * gains[l]
-        ).astype(BF16)
-        grad_in = contract_rows(normed, ag_b[l, :, :R])
-        grad_out = contract_rows(ag_f[l, :, :R], incoming[...])
-
+    def pass_grad(l, grad, own, outgoing, arriving, ssem, rsem):
         @pl.when(q == l)
         def _():
-            gin_ref[...] = grad_in
-            gout_ref[...] = grad_out
+            own[...] = grad
 
         @pl.when(q != l)
         def _():
-            gi_send[l] = grad_in.astype(BF16)
-            go_send[l] = grad_out.astype(BF16)
+            outgoing[l] = grad.astype(BF16)
             slot = lax.rem(q - l - 1 + 2 * S, S)
-            send(gi_send.at[l], gi_recv.at[slot], g_send, g_recv, l, d)
-            send(go_send.at[l], go_recv.at[slot], h_send, h_recv, l, d)
+            send(outgoing.at[l], arriving.at[slot], ssem, rsem, l, d)
+
+    def send_grad_in(l):
+        inv = join_halves(ag_b[l], R + R // 2, R // 4)
+        normed = (xs[layer_rows(l), :].astype(F32) * inv * gains[l]).astype(BF16)
+        grad_in = contract_rows(normed, ag_b[l, :, :R])
+        pass_grad(l, grad_in, gin_ref, gi_send, gi_recv, g_send, g_recv)
+
+    def send_grad_out(l, incoming):
+        grad_out = contract_rows(ag_f[l], incoming[...])
+        pass_grad(l, grad_out, gout_ref, go_send, go_recv, h_send, h_recv)
 
     for step in range(S):
         l = S - 1 - step
@@ -236,10 +256,10 @@
         pay_b[l] = part.astype(BF16)
         exchange(lambda peer: pay_b.at[l, rows(peer), :], rs_b.at[l], pb_s.at[l], pb_r.at[l])
         rs_b[l, rows(d), :] = pay_b[l, rows(d), :]
-        if step == 0:
-            send_outputs(S - 1)
-        else:
-            send_grads(l + 1, cot if step == 1 else delta.at[step - 2])
+        send_bulk()
+        send_grad_out(l, incoming)
+        if step > 0:
+            send_grad_in(l + 1)
         wait_bytes(rs_b.at[l, head], pb_r.at[l])
         total = rs_b[l, 0:rb, :].astype(F32)
         for b in range(1, DP):
@@ -249,21 +269,24 @@
         inv = inv_keep[l][:, 0:1]
         mean = jnp.sum(d_pre.astype(F32) * sum_keep[l], axis=1, keepdims=True) / D
         ag_b[l, rows(d), :] = jnp.concatenate(
-            [d_pre, split_halves(inv * inv * inv * mean, R // 2)], axis=1
+            [d_pre, split_halves(inv * inv * inv * mean, R // 4), split_halves(inv, R // 4)],
+            axis=1,
         )
         exchange(lambda peer: ag_b.at[l, rows(d), :], ag_b.at[l], ab_s.at[l], ab_r.at[l])
+        send_bulk()
         wait_bytes(ag_b.at[l, head], ab_r.at[l])
 
         if l > 0:
             scaled = contract_last(ag_b[l, :, :R], wi[l]) * gains[l]
             delta[step] = (
                 incoming[...].astype(F32)
-                + join_halves(ag_f[l], R) * scaled
-                - xs[layer_rows(l), :].astype(F32) * join_halves(ag_b[l], R)
+                + join_halves(ag_b[l], R + R // 2, R // 4) * scaled
+                - xs[layer_rows(l), :].astype(F32) * join_halves(ag_b[l], R, R // 4)
             ).astype(BF16)
 
         if l == 0:
-            send_grads(0, incoming)
+            send_grad_in(0)
+            send_some_out(len(waiting_out))
 
     wait_bytes(gi_recv, g_recv)
     wait_bytes(go_recv, h_recv)
@@ -329,7 +352,7 @@
         pltpu.VMEM((S, R, F), BF16),
         pltpu.VMEM((S, T, 2 * R), BF16),
         pltpu.VMEM((S, T, 2 * R), BF16),
-        pltpu.VMEM((S, T, 2 * R), BF16),
+        pltpu.VMEM((S, T, R), BF16),
         pltpu.VMEM((S, T, R), BF16),
         pltpu.VMEM((S, T, R), BF16),
         pltpu.VMEM((S, T, 2 * R), BF16),
@@ -356,7 +379,7 @@
             jax.ShapeDtypeStruct((R, F), F32),
             jax.ShapeDtypeStruct((8, 128), F32),
         ),
-        in_specs=[any_spec] * 5,
+        in_specs=[any_spec] * 3 + [vmem_spec] * 2,
         out_specs=(any_spec, vmem_spec, vmem_spec, vmem_spec),
         scratch_shapes=scratch,
         compiler_params=pltpu.CompilerParams(
@@ -375,7 +398,7 @@
     rank_width = master_in.shape[2]
     section_rows, shard_in, shard_out, squares = run_stack(
         stack_input, out_cotangent, norm_gain,
-        master_in[0].astype(BF16), master_out[0].astype(BF16),
+        master_in[0], master_out[0],
     )
     total_sq = jnp.sum(squares)
     norm_limit = clip_rms * math.sqrt(2.0 * model_width * rank_width * num_sections)

time: 224 us -> 195 us (0.87)
  Pallas kernels: 209 us -> 185 us
  other arithmetic: 10.5 us -> 6.66 us
    pallas_call x1, Pallas kernels: 209 us -> 185 us  [run_stack(): pl.pallas_call(functools.partial(stack_kernel, S, DP, rb, F, R, D), out_s...]
    convert_element_type x2 -> x0, other arithmetic: 3.84 us -> none  [the longest x1 1.92 us: shards(): master_in[0].astype(BF16)]
where the time goes in v2:
time: 195 us
  Pallas kernels  185 us (95%)
  other arithmetic  6.66 us (3%)
  local copies, waits for them, and re-layouts  2.26 us (1%)
    pallas_call x1, Pallas kernels, run_stack(): pl.pallas_call(functools.partial(stack_kernel, S, DP, rb, F, R, D), out_s...  185 us

profile of v2, /device:TPU:0, one launch (start us, length us, event | category | flops | bytes accessed | tf_op | source)
XLA Modules:
  0.0 195.1 jit_solution(16033067668883084534)
XLA Ops:
  0.6 0.0 copy-start.1
  0.6 0.0 copy-start.3
  0.7 0.0 copy-start.4
  0.7 184.7 %adapter_stack.1 = (bf16[128,12288]{1,0:T(8,128)(2,1)}, f32[1536,128]{1,0:T(8,128)}, f32[128,1536]{1,0:T(8,128)}, f32[8,128]{1,0:T(8,128)}) custom-call(bf16[128,12288]{1,0:T(8,128)(2,1)} %x_hbm.1, bf16[128,12288]{1,0:T(8,128)(2,1)} %cot_hbm.1, f32[1,12288]{1,0:T(1,128)} %gain_hbm.1, f32[1536,128]{1,0:T(8,128)} %bitcast.43, f32[128,1536]{1,0:T(8,128)} %bitcast.42), custom_call_target="tpu_custom_call" | custom-call | tf_op jit(solution)/shard_map/adapter_stack/pallas_call | solution.py:374
  185.4 0.0 copy-start.2
  185.4 1.4 reduce_sum.9
  187.5 0.0 copy-start.5
  187.5 0.0 copy-start.6
  187.5 0.0 copy-start.7
  187.5 0.0 copy-done.1
  187.6 0.0 copy-done.3
  187.6 0.0 copy-done.4
  187.6 3.3 %fusion.4 = (f32[1,128,1536]{2,1,0:T(8,128)}, f32[1,128,1536]{2,1,0:T(8,128)}, f32[1,128,1536]{2,1,0:T(8,128)}) fusion(f32[128,1536]{1,0:T(8,128)} %get-tuple-element.14, f32[]{:T(128)S(6)} %div.33, f32[1,128,1536]{2,1,0:T(8,128)S(1)} %copy-done.3, f32[1,128,1536]{2,1,0:T(8,128)S(1)} %copy-done.4, f32[1,128,1536]{2,1,0:T(8,128)S(1)} %copy-done.1), kind=kLoop, calls=%fused_computation.10 | loop fusion | flops 3145728 | bytes 5505028 | tf_op jit(solution)/shard_map/broadcast_in_dim | solution.py:419
  190.9 0.0 copy-start
  190.9 0.0 copy-done.2
  190.9 0.0 copy-done.5
  190.9 0.0 copy-done.6
  190.9 0.0 copy-done.7
  190.9 2.0 %fusion.5 = (f32[1,1536,128]{2,1,0:T(8,128)}, f32[1,1536,128]{2,1,0:T(8,128)}, f32[1,1536,128]{2,1,0:T(8,128)}) fusion(f32[1536,128]{1,0:T(8,128)S(1)} %copy-done.7, f32[]{:T(128)S(6)} %div.33, f32[1,1536,128]{2,1,0:T(8,128)S(1)} %copy-done.5, f32[1,1536,128]{2,1,0:T(8,128)S(1)} %copy-done.6, f32[1,1536,128]{2,1,0:T(8,128)S(1)} %copy-done.2), kind=kLoop, calls=%fused_computation.11 | loop fusion | flops 3145728 | bytes 5505028 | tf_op jit(solution)/shard_map/broadcast_in_dim | solution.py:418
  192.9 0.6 copy-done
  193.5 1.7 copy.17
Async XLA Ops:
  0.6 186.9 %copy-start.1 = (f32[1,128,1536]{2,1,0:T(8,128)S(1)}, f32[1,128,1536]{2,1,0:T(8,128)}, u32[]{:S(2)}) copy-start(f32[1,128,1536]{2,1,0:T(8,128)} %param.13) | copy-start | bytes 2359300
  0.6 186.9 %copy-start.3 = (f32[1,128,1536]{2,1,0:T(8,128)S(1)}, f32[1,128,1536]{2,1,0:T(8,128)}, u32[]{:S(2)}) copy-start(f32[1,128,1536]{2,1,0:T(8,128)} %param.17) | copy-start | bytes 2359300
  0.7 186.9 %copy-start.4 = (f32[1,128,1536]{2,1,0:T(8,128)S(1)}, f32[1,128,1536]{2,1,0:T(8,128)}, u32[]{:S(2)}) copy-start(f32[1,128,1536]{2,1,0:T(8,128)} %param.15) | copy-start | bytes 2359300
  185.4 5.5 %copy-start.2 = (f32[1,1536,128]{2,1,0:T(8,128)S(1)}, f32[1,1536,128]{2,1,0:T(8,128)}, u32[]{:S(2)}) copy-start(f32[1,1536,128]{2,1,0:T(8,128)} %param.12) | copy-start | bytes 2359300
  187.5 3.4 %copy-start.5 = (f32[1,1536,128]{2,1,0:T(8,128)S(1)}, f32[1,1536,128]{2,1,0:T(8,128)}, u32[]{:S(2)}) copy-start(f32[1,1536,128]{2,1,0:T(8,128)} %param.16) | copy-start | bytes 2359300
  187.5 3.4 %copy-start.6 = (f32[1,1536,128]{2,1,0:T(8,128)S(1)}, f32[1,1536,128]{2,1,0:T(8,128)}, u32[]{:S(2)}) copy-start(f32[1,1536,128]{2,1,0:T(8,128)} %param.14) | copy-start | bytes 2359300
  187.5 3.4 %copy-start.7 = (f32[1536,128]{1,0:T(8,128)S(1)}, f32[1536,128]{1,0:T(8,128)}, u32[]{:S(2)}) copy-start(f32[1536,128]{1,0:T(8,128)} %get-tuple-element.13) | copy-start | bytes 2359300
  190.9 2.6 %copy-start = (bf16[128,12288]{1,0:T(8,128)(2,1)S(1)}, bf16[128,12288]{1,0:T(8,128)(2,1)}, u32[]{:S(2)}) copy-start(bf16[128,12288]{1,0:T(8,128)(2,1)} %get-tuple-element.11) | copy-start | bytes 9437188

commit v3 on v2

--- a/solution.py
+++ b/solution.py
@@ -71,7 +71,7 @@
 
 
 def stack_kernel(
-    S, DP, rb, F, R, D,
+    S, DP, H, rb, F, R, D,
     x_hbm, cot_hbm, gain_hbm, win_ref, wout_ref,
     out_hbm, gin_ref, gout_ref, tot_ref,
     xs, cot, delta, gains, wi, wo,
@@ -87,6 +87,8 @@
     d = lax.axis_index("dp")
     N = S * DP
     T = DP * rb
+    rh = rb // H
+    Th = DP * rh
 
     def place(sec, dp):
         return {"section": sec, "dp": dp}
@@ -100,8 +102,11 @@
     def wait_bytes(ref, sem):
         pltpu.make_async_copy(ref, ref, sem).wait()
 
-    def rows(block):
-        return pl.ds(pl.multiple_of(block * rb, rb), rb)
+    def home_rows(h):
+        return pl.ds(pl.multiple_of(q * rb + h * rh, rh), rh)
+
+    def rows(block, h=0, base=0):
+        return pl.ds(pl.multiple_of(base + h * Th + block * rh, rh), rh)
 
     def cols(block):
         return pl.ds(pl.multiple_of(block * F, 128), F)
@@ -125,12 +130,15 @@
     own_gain.wait()
     pl.semaphore_wait(barrier, N - 1)
 
-    def send_rows(i, src_hbm, dst, ssem, rsem):
+    def send_rows(h, i, src_hbm, dst, ssem, rsem):
+        target = dst.at[rows(d, h), :]
         if i == 0:
-            pltpu.make_async_copy(src_hbm.at[rows(q), cols(d)], dst.at[rows(d), :], rsem).start()
+            src = src_hbm.at[home_rows(h), cols(d)]
+            pltpu.make_async_copy(src, target, rsem.at[h]).start()
         else:
             peer = lax.rem(d + i, DP)
-            send(src_hbm.at[rows(q), cols(peer)], dst.at[rows(d), :], ssem, rsem, q, peer)
+            src = src_hbm.at[home_rows(h), cols(peer)]
+            send(src, target, ssem.at[h], rsem.at[h], q, peer)
 
     def spread_layers(src, dst, ssem, rsem):
         for j in [S // 2] + [k for k in range(1, S) if k != S // 2]:
@@ -141,30 +149,33 @@
         def _():
             wait_bytes(buffer.at[l], rsem.at[l])
 
-    def exchange(src_of, dst, ssem, rsem):
+    def exchange(src_of, target, ssem, rsem):
         def body(i, carry):
             peer = lax.rem(d + i, DP)
-            send(src_of(peer), dst.at[rows(d), :], ssem, rsem, q, peer)
+            send(src_of(peer), target, ssem, rsem, q, peer)
             return carry
 
         lax.fori_loop(1, DP, body, 0)
 
-    head = pl.ds(0, (DP - 1) * rb)
-
-    for i in range(DP):
-        send_rows(i, x_hbm, xs.at[pl.ds(0, T)], x_send, x_recv)
-    spread_layers(gains.at[q], gains, gn_send, gn_recv)
-    spread_layers(wi.at[q], wi, wi_ssem, wi_rsem)
-    wait_bytes(xs.at[pl.ds(0, T)], x_recv)
-    spread_layers(wo.at[q], wo, wo_ssem, wo_rsem)
+    head = pl.ds(0, (DP - 1) * rh)
+
+    for h in range(H):
+        for i in range(DP):
+            send_rows(h, i, x_hbm, xs.at[pl.ds(0, T)], x_send, x_recv)
+        if h == 0:
+            spread_layers(gains.at[q], gains, gn_send, gn_recv)
+            spread_layers(wi.at[q], wi, wi_ssem, wi_rsem)
 
     def layer_rows(l):
         return pl.ds(l * T, T)
 
-    def send_output(l, i):
+    def stream_rows(h, l=0):
+        return pl.ds(l * T + h * Th, Th)
+
+    def send_output(l, h, i):
         peer = lax.rem(d + i, DP)
-        block = xs.at[pl.ds(pl.multiple_of((l + 1) * T + peer * rb, rb), rb), :]
-        target = out_hbm.at[rows(q), cols(d)]
+        block = xs.at[rows(peer, h, (l + 1) * T), :]
+        target = out_hbm.at[home_rows(h), cols(d)]
         if i > 0:
             send(block, target, o_send, o_recv, l, peer)
             return
@@ -177,12 +188,12 @@
         def _():
             pltpu.make_async_copy(block, target, o_recv).start()
 
-    waiting_cot = list(range(DP))
+    waiting_cot = [(h, i) for h in range(H) for i in range(DP)]
     waiting_out = []
 
     def send_some_cot(count):
         for _ in range(min(count, len(waiting_cot))):
-            send_rows(waiting_cot.pop(0), cot_hbm, cot, c_send, c_recv)
+            send_rows(*waiting_cot.pop(0), cot_hbm, cot, c_send, c_recv)
 
     def send_some_out(count):
         for _ in range(min(count, len(waiting_out))):
@@ -190,43 +201,73 @@
 
     def send_bulk():
         if waiting_cot:
-            send_some_cot(-(-DP // 4))
+            send_some_cot(-(-DP // S))
         else:
-            send_some_out(-(-DP * S // (3 * S - 1)))
-
-    for l in range(S):
-        wait_layer(gains, gn_recv, l)
-        wait_layer(wi, wi_rsem, l)
-        wide = xs[layer_rows(l), :].astype(F32)
+            send_some_out(-(-DP // 3))
+
+    def add_blocks(buffer, k):
+        total = buffer[k, 0:rh, :].astype(F32)
+        for b in range(1, DP):
+            total = total + buffer[k, b * rh : (b + 1) * rh, :].astype(F32)
+        return total
+
+    def forward_partial(l, h):
+        k = l * H + h
+        if l == 0:
+            wait_bytes(xs.at[stream_rows(h)], x_recv.at[h])
+        if h == 0:
+            wait_layer(gains, gn_recv, l)
+            wait_layer(wi, wi_rsem, l)
+        wide = xs[stream_rows(h, l), :].astype(F32)
         part = jnp.dot((wide * gains[l]).astype(BF16), wi[l], preferred_element_type=F32)
         squares = jnp.sum(wide * wide, axis=1, keepdims=True)
-        pay_f[l] = jnp.concatenate([part.astype(BF16), split_halves(squares, R // 2)], axis=1)
-        exchange(lambda peer: pay_f.at[l, rows(peer), :], rs_f.at[l], pf_s.at[l], pf_r.at[l])
-        rs_f[l, rows(d), :] = pay_f[l, rows(d), :]
-        send_bulk()
-        wait_bytes(rs_f.at[l, head], pf_r.at[l])
-        total = rs_f[l, 0:rb, :].astype(F32)
-        for b in range(1, DP):
-            total = total + rs_f[l, b * rb : (b + 1) * rb, :].astype(F32)
+        pay_f[k] = jnp.concatenate([part.astype(BF16), split_halves(squares, R // 2)], axis=1)
+        exchange(
+            lambda peer: pay_f.at[k, rows(peer), :], rs_f.at[k, rows(d), :], pf_s.at[k], pf_r.at[k]
+        )
+        rs_f[k, rows(d), :] = pay_f[k, rows(d), :]
+
+    def forward_act(l, h):
+        k = l * H + h
+        wait_bytes(rs_f.at[k, head], pf_r.at[k])
+        total = add_blocks(rs_f, k)
         inv = lax.rsqrt(join_halves(total, R, R // 2) / D + norm_eps)
         pre = total[:, :R] * inv
         act, _ = gelu_pair(pre)
-        pre_keep[l] = pre
-        sum_keep[l] = total[:, :R]
-        inv_keep[l] = jnp.broadcast_to(inv, (rb, R))
-        ag_f[l, rows(d), :] = act.astype(BF16)
-        exchange(lambda peer: ag_f.at[l, rows(d), :], ag_f.at[l], af_s.at[l], af_r.at[l])
+        mine = ag_f.at[l, rows(d, h), :]
+        mine[...] = act.astype(BF16)
+        exchange(lambda peer: mine, mine, af_s.at[k], af_r.at[k])
+        pre_keep[k] = pre
+        sum_keep[k] = total[:, :R]
+        inv_keep[k] = jnp.broadcast_to(inv, (rh, R))
+
+    def forward_add(l, h):
+        k = l * H + h
+        if h == 0:
+            wait_layer(wo, wo_rsem, l)
+        wait_bytes(ag_f.at[l, head], af_r.at[k])
+        xs[stream_rows(h, l + 1), :] = (
+            xs[stream_rows(h, l), :].astype(F32)
+            + jnp.dot(ag_f[l, stream_rows(h), :], wo[l], preferred_element_type=F32)
+        ).astype(BF16)
+        waiting_out.extend((l, h, i) for i in range(DP))
+
+    for h in range(H):
+        forward_partial(0, h)
+        if h == 0:
+            spread_layers(wo.at[q], wo, wo_ssem, wo_rsem)
         send_bulk()
-        wait_layer(wo, wo_rsem, l)
-        wait_bytes(ag_f.at[l, head], af_r.at[l])
-        xs[layer_rows(l + 1), :] = (
-            xs[layer_rows(l), :].astype(F32)
-            + jnp.dot(ag_f[l], wo[l], preferred_element_type=F32)
-        ).astype(BF16)
-        waiting_out.extend((l, i) for i in range(DP))
-
-    send_some_cot(DP)
-    wait_bytes(cot, c_recv)
+    for l in range(S):
+        for h in range(H):
+            forward_act(l, h)
+            send_bulk()
+        for h in range(H):
+            forward_add(l, h)
+            if l + 1 < S:
+                forward_partial(l + 1, h)
+                send_bulk()
+
+    send_some_cot(DP * H)
 
     def pass_grad(l, grad, own, outgoing, arriving, ssem, rsem):
         @pl.when(q == l)
@@ -249,44 +290,63 @@
         grad_out = contract_rows(ag_f[l], incoming[...])
         pass_grad(l, grad_out, gout_ref, go_send, go_recv, h_send, h_recv)
 
-    for step in range(S):
-        l = S - 1 - step
-        incoming = cot if step == 0 else delta.at[step - 1]
-        part = contract_last(incoming[...], wo[l])
-        pay_b[l] = part.astype(BF16)
-        exchange(lambda peer: pay_b.at[l, rows(peer), :], rs_b.at[l], pb_s.at[l], pb_r.at[l])
-        rs_b[l, rows(d), :] = pay_b[l, rows(d), :]
-        send_bulk()
-        send_grad_out(l, incoming)
-        if step > 0:
-            send_grad_in(l + 1)
-        wait_bytes(rs_b.at[l, head], pb_r.at[l])
-        total = rs_b[l, 0:rb, :].astype(F32)
-        for b in range(1, DP):
-            total = total + rs_b[l, b * rb : (b + 1) * rb, :].astype(F32)
-        _, slope = gelu_pair(pre_keep[l])
-        d_pre = (total * slope).astype(BF16)
-        inv = inv_keep[l][:, 0:1]
-        mean = jnp.sum(d_pre.astype(F32) * sum_keep[l], axis=1, keepdims=True) / D
-        ag_b[l, rows(d), :] = jnp.concatenate(
+    def incoming(l):
+        return cot if l == S - 1 else delta.at[l]
+
+    def backward_partial(l, h):
+        k = l * H + h
+        if l == S - 1:
+            wait_bytes(cot.at[stream_rows(h)], c_recv.at[h])
+        part = contract_last(incoming(l)[stream_rows(h), :], wo[l])
+        pay_b[k] = part.astype(BF16)
+        exchange(
+            lambda peer: pay_b.at[k, rows(peer), :], rs_b.at[k, rows(d), :], pb_s.at[k], pb_r.at[k]
+        )
+        rs_b[k, rows(d), :] = pay_b[k, rows(d), :]
+
+    def backward_slope(l, h):
+        k = l * H + h
+        _, slope = gelu_pair(pre_keep[k])
+        inv = inv_keep[k][:, 0:1]
+        wait_bytes(rs_b.at[k, head], pb_r.at[k])
+        d_pre = (add_blocks(rs_b, k) * slope).astype(BF16)
+        mean = jnp.sum(d_pre.astype(F32) * sum_keep[k], axis=1, keepdims=True) / D
+        mine = ag_b.at[l, rows(d, h), :]
+        mine[...] = jnp.concatenate(
             [d_pre, split_halves(inv * inv * inv * mean, R // 4), split_halves(inv, R // 4)],
             axis=1,
         )
-        exchange(lambda peer: ag_b.at[l, rows(d), :], ag_b.at[l], ab_s.at[l], ab_r.at[l])
+        exchange(lambda peer: mine, mine, ab_s.at[k], ab_r.at[k])
+
+    def backward_add(l, h):
+        wait_bytes(ag_b.at[l, head], ab_r.at[l * H + h])
+        if l == 0:
+            return
+        gathered = ag_b[l, stream_rows(h), :]
+        scaled = contract_last(gathered[:, :R], wi[l]) * gains[l]
+        delta[l - 1, stream_rows(h), :] = (
+            incoming(l)[stream_rows(h), :].astype(F32)
+            + join_halves(gathered, R + R // 2, R // 4) * scaled
+            - xs[stream_rows(h, l), :].astype(F32) * join_halves(gathered, R, R // 4)
+        ).astype(BF16)
+
+    for h in range(H):
+        backward_partial(S - 1, h)
         send_bulk()
-        wait_bytes(ag_b.at[l, head], ab_r.at[l])
-
-        if l > 0:
-            scaled = contract_last(ag_b[l, :, :R], wi[l]) * gains[l]
-            delta[step] = (
-                incoming[...].astype(F32)
-                + join_halves(ag_b[l], R + R // 2, R // 4) * scaled
-                - xs[layer_rows(l), :].astype(F32) * join_halves(ag_b[l], R, R // 4)
-            ).astype(BF16)
-
-        if l == 0:
-            send_grad_in(0)
-            send_some_out(len(waiting_out))
+    for l in range(S - 1, -1, -1):
+        send_grad_out(l, incoming(l))
+        for h in range(H):
+            backward_slope(l, h)
+            send_bulk()
+        if l + 1 < S:
+            send_grad_in(l + 1)
+        for h in range(H):
+            backward_add(l, h)
+            if l > 0:
+                backward_partial(l - 1, h)
+                send_bulk()
+    send_grad_in(0)
+    send_some_out(len(waiting_out))
 
     wait_bytes(gi_recv, g_recv)
     wait_bytes(go_recv, h_recv)
@@ -317,19 +377,20 @@
 
     wait_bytes(out_hbm, o_recv)
     wait_bytes(xs.at[pl.ds(0, (N - 1) * rb)], o_send)
-    wait_bytes(xs.at[head], x_send)
-    wait_bytes(xs.at[head], c_send)
+    for h in range(H):
+        wait_bytes(xs.at[head], x_send.at[h])
+        wait_bytes(xs.at[head], c_send.at[h])
     wait_bytes(gains.at[pl.ds(0, S - 1)], gn_send)
     wait_bytes(wi.at[pl.ds(0, S - 1)], wi_ssem)
     wait_bytes(wo.at[pl.ds(0, S - 1)], wo_ssem)
     wait_bytes(gi_recv, g_send)
     wait_bytes(go_recv, h_send)
     wait_bytes(sq_recv, q_send)
-    for l in range(S):
-        wait_bytes(rs_f.at[l, head], pf_s.at[l])
-        wait_bytes(ag_f.at[l, head], af_s.at[l])
-        wait_bytes(rs_b.at[l, head], pb_s.at[l])
-        wait_bytes(ag_b.at[l, head], ab_s.at[l])
+    for k in range(S * H):
+        wait_bytes(rs_f.at[k, head], pf_s.at[k])
+        wait_bytes(ag_f.at[0, head], af_s.at[k])
+        wait_bytes(rs_b.at[k, head], pb_s.at[k])
+        wait_bytes(ag_b.at[0, head], ab_s.at[k])
 
 
 def run_stack(x, cot, gain, win, wout):
@@ -338,6 +399,7 @@
     tok, D = x.shape
     F, R = win.shape
     rb = tok // S
+    H = 2 if rb % 32 == 0 else 1
     T = DP * rb
     N = S * DP
     sem = pltpu.SemaphoreType.DMA
@@ -350,29 +412,29 @@
         pltpu.VMEM((S, 1, F), F32),
         pltpu.VMEM((S, F, R), BF16),
         pltpu.VMEM((S, R, F), BF16),
+        pltpu.VMEM((S * H, T // H, 2 * R), BF16),
+        pltpu.VMEM((S * H, T // H, 2 * R), BF16),
+        pltpu.VMEM((S, T, R), BF16),
+        pltpu.VMEM((S * H, T // H, R), BF16),
+        pltpu.VMEM((S * H, T // H, R), BF16),
         pltpu.VMEM((S, T, 2 * R), BF16),
-        pltpu.VMEM((S, T, 2 * R), BF16),
-        pltpu.VMEM((S, T, R), BF16),
-        pltpu.VMEM((S, T, R), BF16),
-        pltpu.VMEM((S, T, R), BF16),
-        pltpu.VMEM((S, T, 2 * R), BF16),
-        pltpu.VMEM((S, rb, R), F32),
-        pltpu.VMEM((S, rb, R), F32),
-        pltpu.VMEM((S, rb, R), F32),
+        pltpu.VMEM((S * H, rb // H, R), F32),
+        pltpu.VMEM((S * H, rb // H, R), F32),
+        pltpu.VMEM((S * H, rb // H, R), F32),
         pltpu.VMEM((S, F, R), BF16),
         pltpu.VMEM((S, R, F), BF16),
         pltpu.VMEM((S - 1, F, R), BF16),
         pltpu.VMEM((S - 1, R, F), BF16),
         pltpu.VMEM((8, 128), F32),
         pltpu.VMEM(((N - 1) * 8, 128), F32),
-        sem, sem, sem, sem, sem, sem((S,)),
+        sem((H,)), sem((H,)), sem((H,)), sem((H,)), sem, sem((S,)),
         sem, sem((S,)), sem, sem((S,)),
-        sem((S,)), sem((S,)), sem((S,)), sem((S,)),
-        sem((S,)), sem((S,)), sem((S,)), sem((S,)),
+        sem((S * H,)), sem((S * H,)), sem((S * H,)), sem((S * H,)),
+        sem((S * H,)), sem((S * H,)), sem((S * H,)), sem((S * H,)),
         sem, sem, sem, sem, sem, sem, sem, sem,
     ]
     return pl.pallas_call(
-        functools.partial(stack_kernel, S, DP, rb, F, R, D),
+        functools.partial(stack_kernel, S, DP, H, rb, F, R, D),
         out_shape=(
             jax.ShapeDtypeStruct((tok, D), BF16),
             jax.ShapeDtypeStruct((F, R), F32),

time: 195 us -> 185 us (0.949)
  Pallas kernels: 185 us -> 174 us
    pallas_call x1, Pallas kernels: 185 us -> 174 us  [run_stack(): pl.pallas_call(functools.partial(stack_kernel, S, DP, H, rb, F, R, D), ou...]
where the time goes in v3:
time: 185 us
  Pallas kernels  174 us (94%)
  other arithmetic  6.66 us (4%)
  local copies, waits for them, and re-layouts  2.26 us (1%)
    pallas_call x1, Pallas kernels, run_stack(): pl.pallas_call(functools.partial(stack_kernel, S, DP, H, rb, F, R, D), ou...  174 us

profile of v3, /device:TPU:0, one launch (start us, length us, event | category | flops | bytes accessed | tf_op | source)
XLA Modules:
  0.0 184.9 jit_solution(6256348197089571362)
XLA Ops:
  0.6 0.0 copy-start.1
  0.6 0.0 copy-start.3
  0.7 0.0 copy-start.4
  0.7 174.5 %adapter_stack.1 = (bf16[128,12288]{1,0:T(8,128)(2,1)}, f32[1536,128]{1,0:T(8,128)}, f32[128,1536]{1,0:T(8,128)}, f32[8,128]{1,0:T(8,128)}) custom-call(bf16[128,12288]{1,0:T(8,128)(2,1)} %x_hbm.1, bf16[128,12288]{1,0:T(8,128)(2,1)} %cot_hbm.1, f32[1,12288]{1,0:T(1,128)} %gain_hbm.1, f32[1536,128]{1,0:T(8,128)} %bitcast.43, f32[128,1536]{1,0:T(8,128)} %bitcast.42), custom_call_target="tpu_custom_call" | custom-call | tf_op jit(solution)/shard_map/adapter_stack/pallas_call | solution.py:436
  175.1 0.0 copy-start.2
  175.1 1.4 reduce_sum.9
  177.2 0.0 copy-start.5
  177.2 0.0 copy-start.6
  177.3 0.0 copy-start.7
  177.3 0.0 copy-done.1
  177.3 0.0 copy-done.3
  177.3 0.0 copy-done.4
  177.3 3.3 %fusion.4 = (f32[1,128,1536]{2,1,0:T(8,128)}, f32[1,128,1536]{2,1,0:T(8,128)}, f32[1,128,1536]{2,1,0:T(8,128)}) fusion(f32[128,1536]{1,0:T(8,128)} %get-tuple-element.14, f32[]{:T(128)S(6)} %div.33, f32[1,128,1536]{2,1,0:T(8,128)S(1)} %copy-done.3, f32[1,128,1536]{2,1,0:T(8,128)S(1)} %copy-done.4, f32[1,128,1536]{2,1,0:T(8,128)S(1)} %copy-done.1), kind=kLoop, calls=%fused_computation.10 | loop fusion | flops 3145728 | bytes 5505028 | tf_op jit(solution)/shard_map/broadcast_in_dim | solution.py:481
  180.6 0.0 copy-start
  180.6 0.0 copy-done.2
  180.6 0.0 copy-done.5
  180.6 0.0 copy-done.6
  180.6 0.0 copy-done.7
  180.6 2.0 %fusion.5 = (f32[1,1536,128]{2,1,0:T(8,128)}, f32[1,1536,128]{2,1,0:T(8,128)}, f32[1,1536,128]{2,1,0:T(8,128)}) fusion(f32[1536,128]{1,0:T(8,128)S(1)} %copy-done.7, f32[]{:T(128)S(6)} %div.33, f32[1,1536,128]{2,1,0:T(8,128)S(1)} %copy-done.5, f32[1,1536,128]{2,1,0:T(8,128)S(1)} %copy-done.6, f32[1,1536,128]{2,1,0:T(8,128)S(1)} %copy-done.2), kind=kLoop, calls=%fused_computation.11 | loop fusion | flops 3145728 | bytes 5505028 | tf_op jit(solution)/shard_map/broadcast_in_dim | solution.py:480
  182.6 0.6 copy-done
  183.2 1.7 copy.17
Async XLA Ops:
  0.6 176.6 %copy-start.1 = (f32[1,128,1536]{2,1,0:T(8,128)S(1)}, f32[1,128,1536]{2,1,0:T(8,128)}, u32[]{:S(2)}) copy-start(f32[1,128,1536]{2,1,0:T(8,128)} %param.13) | copy-start | bytes 2359300
  0.6 176.6 %copy-start.3 = (f32[1,128,1536]{2,1,0:T(8,128)S(1)}, f32[1,128,1536]{2,1,0:T(8,128)}, u32[]{:S(2)}) copy-start(f32[1,128,1536]{2,1,0:T(8,128)} %param.17) | copy-start | bytes 2359300
  0.7 176.6 %copy-start.4 = (f32[1,128,1536]{2,1,0:T(8,128)S(1)}, f32[1,128,1536]{2,1,0:T(8,128)}, u32[]{:S(2)}) copy-start(f32[1,128,1536]{2,1,0:T(8,128)} %param.15) | copy-start | bytes 2359300
  175.1 5.5 %copy-start.2 = (f32[1,1536,128]{2,1,0:T(8,128)S(1)}, f32[1,1536,128]{2,1,0:T(8,128)}, u32[]{:S(2)}) copy-start(f32[1,1536,128]{2,1,0:T(8,128)} %param.12) | copy-start | bytes 2359300
  177.2 3.4 %copy-start.5 = (f32[1,1536,128]{2,1,0:T(8,128)S(1)}, f32[1,1536,128]{2,1,0:T(8,128)}, u32[]{:S(2)}) copy-start(f32[1,1536,128]{2,1,0:T(8,128)} %param.16) | copy-start | bytes 2359300
  177.2 3.4 %copy-start.6 = (f32[1,1536,128]{2,1,0:T(8,128)S(1)}, f32[1,1536,128]{2,1,0:T(8,128)}, u32[]{:S(2)}) copy-start(f32[1,1536,128]{2,1,0:T(8,128)} %param.14) | copy-start | bytes 2359300
  177.3 3.4 %copy-start.7 = (f32[1536,128]{1,0:T(8,128)S(1)}, f32[1536,128]{1,0:T(8,128)}, u32[]{:S(2)}) copy-start(f32[1536,128]{1,0:T(8,128)} %get-tuple-element.13) | copy-start | bytes 2359300
  180.6 2.6 %copy-start = (bf16[128,12288]{1,0:T(8,128)(2,1)S(1)}, bf16[128,12288]{1,0:T(8,128)(2,1)}, u32[]{:S(2)}) copy-start(bf16[128,12288]{1,0:T(8,128)(2,1)} %get-tuple-element.11) | copy-start | bytes 9437188

commit v4 on v3

--- a/solution.py
+++ b/solution.py
@@ -71,16 +71,18 @@
 
 
 def stack_kernel(
-    S, DP, H, rb, F, R, D,
+    S, DP, H, M, rb, F, R, D,
     x_hbm, cot_hbm, gain_hbm, win_ref, wout_ref,
     out_hbm, gin_ref, gout_ref, tot_ref,
     xs, cot, delta, gains, wi, wo,
     pay_f, rs_f, ag_f, pay_b, rs_b, ag_b,
     pre_keep, sum_keep, inv_keep,
     gi_send, go_send, gi_recv, go_recv, sq_send, sq_recv,
+    near_x, near_w, near_act,
     x_send, x_recv, c_send, c_recv, gn_send, gn_recv,
     wi_ssem, wi_rsem, wo_ssem, wo_rsem,
     pf_s, pf_r, af_s, af_r, pb_s, pb_r, ab_s, ab_r,
+    nx_s, nx_r, nw_s, nw_r, na_s, na_r,
     o_send, o_recv, g_send, g_recv, h_send, h_recv, q_send, q_recv,
 ):
     q = lax.axis_index("section")
@@ -188,6 +190,87 @@
         def _():
             pltpu.make_async_copy(block, target, o_recv).start()
 
+    near = M > 1
+    tok = S * rb
+    Z = DP // M
+    Fs = F // S
+    group = d // M
+    member = lax.rem(d, M)
+
+    def near_cols(g):
+        return pl.ds(pl.multiple_of((g * M + member) * F + q * Fs, 128), Fs)
+
+    def mate_cols(g, mate):
+        return pl.ds(pl.multiple_of((g * M + mate) * F + q * Fs, 128), Fs)
+
+    def near_rows(m):
+        return pl.ds(pl.multiple_of(m * tok, tok), tok)
+
+    def send_near_x():
+        for g in range(Z):
+            target = near_x.at[0, g, near_rows(member), :]
+            pltpu.make_async_copy(x_hbm.at[:, near_cols(g)], target, nx_r).start()
+            for j in range(1, M):
+                mate = lax.rem(member + j, M)
+                src = x_hbm.at[:, mate_cols(g, mate)]
+                send(src, target, nx_s, nx_r, q, group * M + mate)
+
+    def send_near_w(l, j):
+        share = wo.at[l, :, pl.ds(pl.multiple_of(q * Fs, 128), Fs)]
+        target = near_w.at[l, group]
+        if j == 0:
+            pltpu.make_async_copy(share, target, nw_r.at[l]).start()
+        else:
+            other = lax.rem(group + j, Z)
+            send(share, target, nw_s.at[l], nw_r.at[l], q, other * M + member)
+
+    def send_near_act(l, h, mine):
+        target = near_act.at[
+            l, pl.ds(pl.multiple_of(member * tok + q * rb + h * rh, rh), rh), :
+        ]
+        target[...] = mine[...]
+
+        def body(j, carry):
+            sec = lax.rem(q + j // M, S)
+            mate = lax.rem(member + lax.rem(j, M), M)
+            send(target, target, na_s.at[l], na_r.at[l], sec, group * M + mate)
+            return carry
+
+        lax.fori_loop(1, S * M, body, 0)
+
+    def rebuild(l):
+        if not near:
+            return
+        while waiting_w and waiting_w[0][0] <= l:
+            send_near_w(*waiting_w.pop(0))
+        if l == 0:
+            wait_bytes(near_x.at[0], nx_r)
+        wait_bytes(near_w.at[l], nw_r.at[l])
+        wait_bytes(near_act.at[l, pl.ds(0, (S * M - 1) * rb), :], na_r.at[l])
+        for g in range(Z):
+            near_x[l + 1, g] = (
+                near_x[l, g].astype(F32)
+                + jnp.dot(near_act[l], near_w[l, g], preferred_element_type=F32)
+            ).astype(BF16)
+        waiting_out.extend((l, g, j) for g in range(Z) for j in range(M))
+
+    def send_near_output(l, g, j):
+        mate = lax.rem(member + j, M)
+        block = near_x.at[l + 1, g, near_rows(mate), :]
+        target = out_hbm.at[:, near_cols(g)]
+        if j > 0:
+            send(block, target, o_send, o_recv, l, group * M + mate)
+            return
+
+        @pl.when(q != l)
+        def _():
+            send(block, target, o_send, o_recv, l, d)
+
+        @pl.when(q == l)
+        def _():
+            pltpu.make_async_copy(block, target, o_recv).start()
+
+    waiting_w = []
     waiting_cot = [(h, i) for h in range(H) for i in range(DP)]
     waiting_out = []
 
@@ -197,11 +280,14 @@
 
     def send_some_out(count):
         for _ in range(min(count, len(waiting_out))):
-            send_output(*waiting_out.pop(0))
+            (send_near_output if near else send_output)(*waiting_out.pop(0))
 
     def send_bulk():
         if waiting_cot:
             send_some_cot(-(-DP // S))
+        elif waiting_w:
+            for _ in range(min(3, len(waiting_w))):
+                send_near_w(*waiting_w.pop(0))
         else:
             send_some_out(-(-DP // 3))
 
@@ -237,6 +323,8 @@
         mine = ag_f.at[l, rows(d, h), :]
         mine[...] = act.astype(BF16)
         exchange(lambda peer: mine, mine, af_s.at[k], af_r.at[k])
+        if near:
+            send_near_act(l, h, mine)
         pre_keep[k] = pre
         sum_keep[k] = total[:, :R]
         inv_keep[k] = jnp.broadcast_to(inv, (rh, R))
@@ -245,22 +333,29 @@
         k = l * H + h
         if h == 0:
             wait_layer(wo, wo_rsem, l)
+            if near:
+                waiting_w.extend((l, j) for j in range(Z))
         wait_bytes(ag_f.at[l, head], af_r.at[k])
         xs[stream_rows(h, l + 1), :] = (
             xs[stream_rows(h, l), :].astype(F32)
             + jnp.dot(ag_f[l, stream_rows(h), :], wo[l], preferred_element_type=F32)
         ).astype(BF16)
-        waiting_out.extend((l, h, i) for i in range(DP))
+        if not near:
+            waiting_out.extend((l, h, i) for i in range(DP))
 
     for h in range(H):
         forward_partial(0, h)
         if h == 0:
             spread_layers(wo.at[q], wo, wo_ssem, wo_rsem)
+            if near:
+                send_near_x()
         send_bulk()
     for l in range(S):
         for h in range(H):
             forward_act(l, h)
             send_bulk()
+        if l > 1:
+            rebuild(l - 2)
         for h in range(H):
             forward_add(l, h)
             if l + 1 < S:
@@ -340,6 +435,8 @@
             send_bulk()
         if l + 1 < S:
             send_grad_in(l + 1)
+        if l > S - 3:
+            rebuild(S - 2 + S - 1 - l)
         for h in range(H):
             backward_add(l, h)
             if l > 0:
@@ -376,7 +473,12 @@
     tot_ref[...] = sq + jnp.sum(sq_recv[...].reshape(N - 1, 8, 128), axis=0)
 
     wait_bytes(out_hbm, o_recv)
-    wait_bytes(xs.at[pl.ds(0, (N - 1) * rb)], o_send)
+    wait_bytes(xs.at[pl.ds(0, (N - (Z if near else 1)) * rb)], o_send)
+    if near:
+        wait_bytes(near_x.at[0, :, pl.ds(0, (M - 1) * tok), :], nx_s)
+        for l in range(S):
+            wait_bytes(near_w.at[l, pl.ds(0, Z - 1)], nw_s.at[l])
+            wait_bytes(near_act.at[l, pl.ds(0, (S * M - 1) * rb), :], na_s.at[l])
     for h in range(H):
         wait_bytes(xs.at[head], x_send.at[h])
         wait_bytes(xs.at[head], c_send.at[h])
@@ -400,6 +502,10 @@
     F, R = win.shape
     rb = tok // S
     H = 2 if rb % 32 == 0 else 1
+    M = 2 if DP % 2 == 0 and F % (128 * S) == 0 else 1
+    Z = DP // M
+    Fs = F // S if M > 1 else 128
+    near = (S, Z, M * tok) if M > 1 else (1, 1, 16)
     T = DP * rb
     N = S * DP
     sem = pltpu.SemaphoreType.DMA
@@ -427,14 +533,18 @@
         pltpu.VMEM((S - 1, R, F), BF16),
         pltpu.VMEM((8, 128), F32),
         pltpu.VMEM(((N - 1) * 8, 128), F32),
+        pltpu.VMEM((near[0] + 1, near[1], near[2], Fs), BF16),
+        pltpu.VMEM((near[0], near[1], R, Fs), BF16),
+        pltpu.VMEM((near[0], near[2], R), BF16),
         sem((H,)), sem((H,)), sem((H,)), sem((H,)), sem, sem((S,)),
         sem, sem((S,)), sem, sem((S,)),
         sem((S * H,)), sem((S * H,)), sem((S * H,)), sem((S * H,)),
         sem((S * H,)), sem((S * H,)), sem((S * H,)), sem((S * H,)),
+        sem, sem, sem((S,)), sem((S,)), sem((S,)), sem((S,)),
         sem, sem, sem, sem, sem, sem, sem, sem,
     ]
     return pl.pallas_call(
-        functools.partial(stack_kernel, S, DP, H, rb, F, R, D),
+        functools.partial(stack_kernel, S, DP, H, M, rb, F, R, D),
         out_shape=(
             jax.ShapeDtypeStruct((tok, D), BF16),
             jax.ShapeDtypeStruct((F, R), F32),

time: 185 us -> 189 us (1.022)
  Pallas kernels: 174 us -> 178 us
    pallas_call x1, Pallas kernels: 174 us -> 178 us  [run_stack(): pl.pallas_call(functools.partial(stack_kernel, S, DP, H, M, rb, F, R, D),...]
where the time goes in v4:
time: 189 us; the launch traced here: 188 us
  Pallas kernels  178 us (94%)
  other arithmetic  6.66 us (4%)
  local copies, waits for them, and re-layouts  2.26 us (1%)
    pallas_call x1, Pallas kernels, run_stack(): pl.pallas_call(functools.partial(stack_kernel, S, DP, H, M, rb, F, R, D),...  178 us

profile of v4, /device:TPU:0, one launch (start us, length us, event | category | flops | bytes accessed | tf_op | source)
XLA Modules:
  0.0 188.4 jit_solution(14197292993323544782)
XLA Ops:
  0.6 0.0 copy-start.1
  0.6 0.0 copy-start.3
  0.7 0.0 copy-start.4
  0.7 178.0 %adapter_stack.1 = (bf16[128,12288]{1,0:T(8,128)(2,1)}, f32[1536,128]{1,0:T(8,128)}, f32[128,1536]{1,0:T(8,128)}, f32[8,128]{1,0:T(8,128)}) custom-call(bf16[128,12288]{1,0:T(8,128)(2,1)} %x_hbm.1, bf16[128,12288]{1,0:T(8,128)(2,1)} %cot_hbm.1, f32[1,12288]{1,0:T(1,128)} %gain_hbm.1, f32[1536,128]{1,0:T(8,128)} %bitcast.43, f32[128,1536]{1,0:T(8,128)} %bitcast.42), custom_call_target="tpu_custom_call" | custom-call | tf_op jit(solution)/shard_map/adapter_stack/pallas_call | solution.py:546
  178.7 0.0 copy-start.2
  178.7 1.4 reduce_sum.9
  180.8 0.0 copy-start.5
  180.8 0.0 copy-start.6
  180.8 0.0 copy-start.7
  180.8 0.0 copy-done.1
  180.9 0.0 copy-done.3
  180.9 0.0 copy-done.4
  180.9 3.3 %fusion.4 = (f32[1,128,1536]{2,1,0:T(8,128)}, f32[1,128,1536]{2,1,0:T(8,128)}, f32[1,128,1536]{2,1,0:T(8,128)}) fusion(f32[128,1536]{1,0:T(8,128)} %get-tuple-element.14, f32[]{:T(128)S(6)} %div.33, f32[1,128,1536]{2,1,0:T(8,128)S(1)} %copy-done.3, f32[1,128,1536]{2,1,0:T(8,128)S(1)} %copy-done.4, f32[1,128,1536]{2,1,0:T(8,128)S(1)} %copy-done.1), kind=kLoop, calls=%fused_computation.10 | loop fusion | flops 3145728 | bytes 5505028 | tf_op jit(solution)/shard_map/broadcast_in_dim | solution.py:591
  184.2 0.0 copy-start
  184.2 0.0 copy-done.2
  184.2 0.0 copy-done.5
  184.2 0.0 copy-done.6
  184.2 0.0 copy-done.7
  184.2 2.0 %fusion.5 = (f32[1,1536,128]{2,1,0:T(8,128)}, f32[1,1536,128]{2,1,0:T(8,128)}, f32[1,1536,128]{2,1,0:T(8,128)}) fusion(f32[1536,128]{1,0:T(8,128)S(1)} %copy-done.7, f32[]{:T(128)S(6)} %div.33, f32[1,1536,128]{2,1,0:T(8,128)S(1)} %copy-done.5, f32[1,1536,128]{2,1,0:T(8,128)S(1)} %copy-done.6, f32[1,1536,128]{2,1,0:T(8,128)S(1)} %copy-done.2), kind=kLoop, calls=%fused_computation.11 | loop fusion | flops 3145728 | bytes 5505028 | tf_op jit(solution)/shard_map/broadcast_in_dim | solution.py:590
  186.2 0.6 copy-done
  186.8 1.7 copy.17
Async XLA Ops:
  0.6 180.2 %copy-start.1 = (f32[1,128,1536]{2,1,0:T(8,128)S(1)}, f32[1,128,1536]{2,1,0:T(8,128)}, u32[]{:S(2)}) copy-start(f32[1,128,1536]{2,1,0:T(8,128)} %param.13) | copy-start | bytes 2359300
  0.6 180.2 %copy-start.3 = (f32[1,128,1536]{2,1,0:T(8,128)S(1)}, f32[1,128,1536]{2,1,0:T(8,128)}, u32[]{:S(2)}) copy-start(f32[1,128,1536]{2,1,0:T(8,128)} %param.17) | copy-start | bytes 2359300
  0.7 180.2 %copy-start.4 = (f32[1,128,1536]{2,1,0:T(8,128)S(1)}, f32[1,128,1536]{2,1,0:T(8,128)}, u32[]{:S(2)}) copy-start(f32[1,128,1536]{2,1,0:T(8,128)} %param.15) | copy-start | bytes 2359300
  178.7 5.5 %copy-start.2 = (f32[1,1536,128]{2,1,0:T(8,128)S(1)}, f32[1,1536,128]{2,1,0:T(8,128)}, u32[]{:S(2)}) copy-start(f32[1,1536,128]{2,1,0:T(8,128)} %param.12) | copy-start | bytes 2359300
  180.8 3.4 %copy-start.5 = (f32[1,1536,128]{2,1,0:T(8,128)S(1)}, f32[1,1536,128]{2,1,0:T(8,128)}, u32[]{:S(2)}) copy-start(f32[1,1536,128]{2,1,0:T(8,128)} %param.16) | copy-start | bytes 2359300
  180.8 3.4 %copy-start.6 = (f32[1,1536,128]{2,1,0:T(8,128)S(1)}, f32[1,1536,128]{2,1,0:T(8,128)}, u32[]{:S(2)}) copy-start(f32[1,1536,128]{2,1,0:T(8,128)} %param.14) | copy-start | bytes 2359300
  180.8 3.4 %copy-start.7 = (f32[1536,128]{1,0:T(8,128)S(1)}, f32[1536,128]{1,0:T(8,128)}, u32[]{:S(2)}) copy-start(f32[1536,128]{1,0:T(8,128)} %get-tuple-element.13) | copy-start | bytes 2359300
  184.2 2.6 %copy-start = (bf16[128,12288]{1,0:T(8,128)(2,1)S(1)}, bf16[128,12288]{1,0:T(8,128)(2,1)}, u32[]{:S(2)}) copy-start(bf16[128,12288]{1,0:T(8,128)(2,1)} %get-tuple-element.11) | copy-start | bytes 9437188

commit v5 on v3

--- a/solution.py
+++ b/solution.py
@@ -144,6 +144,24 @@
         for j in [S // 2] + [k for k in range(1, S) if k != S // 2]:
             send(src, dst.at[q], ssem, rsem.at[q], lax.rem(q + j, S), d)
 
+    mate = q + 1 - 2 * lax.rem(q, 2)
+
+    def spread_weights(buffer, ssem, rsem):
+        for j in range(1, S // 2):
+            send(buffer.at[q], buffer.at[q], ssem, rsem.at[q], lax.rem(q + 2 * j, S), d)
+        send(buffer.at[q], buffer.at[q], ssem, rsem.at[q], mate, d)
+
+    def hand_on(buffer, ssem, rsem):
+        for j in range(1, S // 2):
+            l = lax.rem(q + 2 * j, S)
+            wait_bytes(buffer.at[l], rsem.at[l])
+            send(buffer.at[l], buffer.at[l], ssem, rsem.at[l], mate, d)
+
+    def wait_weights(buffer, rsem, l):
+        @pl.when(lax.rem(q + l, 2) == 1)
+        def _():
+            wait_bytes(buffer.at[l], rsem.at[l])
+
     def wait_layer(buffer, rsem, l):
         @pl.when(q != l)
         def _():
@@ -164,7 +182,7 @@
             send_rows(h, i, x_hbm, xs.at[pl.ds(0, T)], x_send, x_recv)
         if h == 0:
             spread_layers(gains.at[q], gains, gn_send, gn_recv)
-            spread_layers(wi.at[q], wi, wi_ssem, wi_rsem)
+            spread_weights(wi, wi_ssem, wi_rsem)
 
     def layer_rows(l):
         return pl.ds(l * T, T)
@@ -217,7 +235,7 @@
             wait_bytes(xs.at[stream_rows(h)], x_recv.at[h])
         if h == 0:
             wait_layer(gains, gn_recv, l)
-            wait_layer(wi, wi_rsem, l)
+            wait_weights(wi, wi_rsem, l)
         wide = xs[stream_rows(h, l), :].astype(F32)
         part = jnp.dot((wide * gains[l]).astype(BF16), wi[l], preferred_element_type=F32)
         squares = jnp.sum(wide * wide, axis=1, keepdims=True)
@@ -244,7 +262,7 @@
     def forward_add(l, h):
         k = l * H + h
         if h == 0:
-            wait_layer(wo, wo_rsem, l)
+            wait_weights(wo, wo_rsem, l)
         wait_bytes(ag_f.at[l, head], af_r.at[k])
         xs[stream_rows(h, l + 1), :] = (
             xs[stream_rows(h, l), :].astype(F32)
@@ -252,11 +270,12 @@
         ).astype(BF16)
         waiting_out.extend((l, h, i) for i in range(DP))
 
+    spread_weights(wo, wo_ssem, wo_rsem)
+    hand_on(wi, wi_ssem, wi_rsem)
     for h in range(H):
         forward_partial(0, h)
-        if h == 0:
-            spread_layers(wo.at[q], wo, wo_ssem, wo_rsem)
         send_bulk()
+    hand_on(wo, wo_ssem, wo_rsem)
     for l in range(S):
         for h in range(H):
             forward_act(l, h)

time: 185 us -> 191 us (1.032)
  Pallas kernels: 174 us -> 180 us
    pallas_call x1, Pallas kernels: 174 us -> 180 us  [run_stack(): pl.pallas_call(functools.partial(stack_kernel, S, DP, H, rb, F, R, D), ou...]
where the time goes in v5:
time: 191 us
  Pallas kernels  180 us (94%)
  other arithmetic  6.66 us (3%)
  local copies, waits for them, and re-layouts  2.26 us (1%)
    pallas_call x1, Pallas kernels, run_stack(): pl.pallas_call(functools.partial(stack_kernel, S, DP, H, rb, F, R, D), ou...  180 us

profile of v5, /device:TPU:0, one launch (start us, length us, event | category | flops | bytes accessed | tf_op | source)
XLA Modules:
  0.0 190.6 jit_solution(5660761743318921592)
XLA Ops:
  0.6 0.0 copy-start.1
  0.6 0.0 copy-start.3
  0.7 0.0 copy-start.4
  0.7 180.2 %adapter_stack.1 = (bf16[128,12288]{1,0:T(8,128)(2,1)}, f32[1536,128]{1,0:T(8,128)}, f32[128,1536]{1,0:T(8,128)}, f32[8,128]{1,0:T(8,128)}) custom-call(bf16[128,12288]{1,0:T(8,128)(2,1)} %x_hbm.1, bf16[128,12288]{1,0:T(8,128)(2,1)} %cot_hbm.1, f32[1,12288]{1,0:T(1,128)} %gain_hbm.1, f32[1536,128]{1,0:T(8,128)} %bitcast.43, f32[128,1536]{1,0:T(8,128)} %bitcast.42), custom_call_target="tpu_custom_call" | custom-call | tf_op jit(solution)/shard_map/adapter_stack/pallas_call | solution.py:455
  180.8 0.0 copy-start.2
  180.8 1.4 reduce_sum.9
  182.9 0.0 copy-start.5
  182.9 0.0 copy-start.6
  183.0 0.0 copy-start.7
  183.0 0.0 copy-done.1
  183.0 0.0 copy-done.3
  183.0 0.0 copy-done.4
  183.0 3.3 %fusion.4 = (f32[1,128,1536]{2,1,0:T(8,128)}, f32[1,128,1536]{2,1,0:T(8,128)}, f32[1,128,1536]{2,1,0:T(8,128)}) fusion(f32[128,1536]{1,0:T(8,128)} %get-tuple-element.14, f32[]{:T(128)S(6)} %div.33, f32[1,128,1536]{2,1,0:T(8,128)S(1)} %copy-done.3, f32[1,128,1536]{2,1,0:T(8,128)S(1)} %copy-done.4, f32[1,128,1536]{2,1,0:T(8,128)S(1)} %copy-done.1), kind=kLoop, calls=%fused_computation.10 | loop fusion | flops 3145728 | bytes 5505028 | tf_op jit(solution)/shard_map/broadcast_in_dim | solution.py:500
  186.3 0.0 copy-start
  186.3 0.0 copy-done.2
  186.3 0.0 copy-done.5
  186.3 0.0 copy-done.6
  186.3 0.0 copy-done.7
  186.3 2.0 %fusion.5 = (f32[1,1536,128]{2,1,0:T(8,128)}, f32[1,1536,128]{2,1,0:T(8,128)}, f32[1,1536,128]{2,1,0:T(8,128)}) fusion(f32[1536,128]{1,0:T(8,128)S(1)} %copy-done.7, f32[]{:T(128)S(6)} %div.33, f32[1,1536,128]{2,1,0:T(8,128)S(1)} %copy-done.5, f32[1,1536,128]{2,1,0:T(8,128)S(1)} %copy-done.6, f32[1,1536,128]{2,1,0:T(8,128)S(1)} %copy-done.2), kind=kLoop, calls=%fused_computation.11 | loop fusion | flops 3145728 | bytes 5505028 | tf_op jit(solution)/shard_map/broadcast_in_dim | solution.py:499
  188.3 0.6 copy-done
  188.9 1.7 copy.17
Async XLA Ops:
  0.6 182.3 %copy-start.1 = (f32[1,128,1536]{2,1,0:T(8,128)S(1)}, f32[1,128,1536]{2,1,0:T(8,128)}, u32[]{:S(2)}) copy-start(f32[1,128,1536]{2,1,0:T(8,128)} %param.13) | copy-start | bytes 2359300
  0.6 182.3 %copy-start.3 = (f32[1,128,1536]{2,1,0:T(8,128)S(1)}, f32[1,128,1536]{2,1,0:T(8,128)}, u32[]{:S(2)}) copy-start(f32[1,128,1536]{2,1,0:T(8,128)} %param.17) | copy-start | bytes 2359300
  0.7 182.3 %copy-start.4 = (f32[1,128,1536]{2,1,0:T(8,128)S(1)}, f32[1,128,1536]{2,1,0:T(8,128)}, u32[]{:S(2)}) copy-start(f32[1,128,1536]{2,1,0:T(8,128)} %param.15) | copy-start | bytes 2359300
  180.8 5.5 %copy-start.2 = (f32[1,1536,128]{2,1,0:T(8,128)S(1)}, f32[1,1536,128]{2,1,0:T(8,128)}, u32[]{:S(2)}) copy-start(f32[1,1536,128]{2,1,0:T(8,128)} %param.12) | copy-start | bytes 2359300
  182.9 3.4 %copy-start.5 = (f32[1,1536,128]{2,1,0:T(8,128)S(1)}, f32[1,1536,128]{2,1,0:T(8,128)}, u32[]{:S(2)}) copy-start(f32[1,1536,128]{2,1,0:T(8,128)} %param.16) | copy-start | bytes 2359300
  182.9 3.4 %copy-start.6 = (f32[1,1536,128]{2,1,0:T(8,128)S(1)}, f32[1,1536,128]{2,1,0:T(8,128)}, u32[]{:S(2)}) copy-start(f32[1,1536,128]{2,1,0:T(8,128)} %param.14) | copy-start | bytes 2359300
  183.0 3.4 %copy-start.7 = (f32[1536,128]{1,0:T(8,128)S(1)}, f32[1536,128]{1,0:T(8,128)}, u32[]{:S(2)}) copy-start(f32[1536,128]{1,0:T(8,128)} %get-tuple-element.13) | copy-start | bytes 2359300
  186.3 2.6 %copy-start = (bf16[128,12288]{1,0:T(8,128)(2,1)S(1)}, bf16[128,12288]{1,0:T(8,128)(2,1)}, u32[]{:S(2)}) copy-start(bf16[128,12288]{1,0:T(8,128)(2,1)} %get-tuple-element.11) | copy-start | bytes 9437188

commit v6 on v3

--- a/solution.py
+++ b/solution.py
@@ -155,7 +155,7 @@
             send(src_of(peer), target, ssem, rsem, q, peer)
             return carry
 
-        lax.fori_loop(1, DP, body, 0)
+        lax.fori_loop(1, DP, body, 0, unroll=DP <= 8)
 
     head = pl.ds(0, (DP - 1) * rh)
 

time: 185 us -> 186 us (level)
  no operation moved by 1% of the time
where the time goes in v6:
time: 186 us; the launch traced here: 185 us
  Pallas kernels  175 us (94%)
  other arithmetic  6.66 us (4%)
  local copies, waits for them, and re-layouts  2.26 us (1%)
    pallas_call x1, Pallas kernels, run_stack(): pl.pallas_call(functools.partial(stack_kernel, S, DP, H, rb, F, R, D), ou...  175 us

profile of v6, /device:TPU:0, one launch (start us, length us, event | category | flops | bytes accessed | tf_op | source)
XLA Modules:
  0.0 185.3 jit_solution(2861718861173314631)
XLA Ops:
  0.6 0.0 copy-start.1
  0.6 0.0 copy-start.3
  0.7 0.0 copy-start.4
  0.7 174.9 %adapter_stack.1 = (bf16[128,12288]{1,0:T(8,128)(2,1)}, f32[1536,128]{1,0:T(8,128)}, f32[128,1536]{1,0:T(8,128)}, f32[8,128]{1,0:T(8,128)}) custom-call(bf16[128,12288]{1,0:T(8,128)(2,1)} %x_hbm.1, bf16[128,12288]{1,0:T(8,128)(2,1)} %cot_hbm.1, f32[1,12288]{1,0:T(1,128)} %gain_hbm.1, f32[1536,128]{1,0:T(8,128)} %bitcast.43, f32[128,1536]{1,0:T(8,128)} %bitcast.42), custom_call_target="tpu_custom_call" | custom-call | tf_op jit(solution)/shard_map/adapter_stack/pallas_call | solution.py:436
  175.6 0.0 copy-start.2
  175.6 1.4 reduce_sum.9
  177.7 0.0 copy-start.5
  177.7 0.0 copy-start.6
  177.7 0.0 copy-start.7
  177.7 0.0 copy-done.1
  177.7 0.0 copy-done.3
  177.7 0.0 copy-done.4
  177.7 3.3 %fusion.4 = (f32[1,128,1536]{2,1,0:T(8,128)}, f32[1,128,1536]{2,1,0:T(8,128)}, f32[1,128,1536]{2,1,0:T(8,128)}) fusion(f32[128,1536]{1,0:T(8,128)} %get-tuple-element.14, f32[]{:T(128)S(6)} %div.33, f32[1,128,1536]{2,1,0:T(8,128)S(1)} %copy-done.3, f32[1,128,1536]{2,1,0:T(8,128)S(1)} %copy-done.4, f32[1,128,1536]{2,1,0:T(8,128)S(1)} %copy-done.1), kind=kLoop, calls=%fused_computation.10 | loop fusion | flops 3145728 | bytes 5505028 | tf_op jit(solution)/shard_map/broadcast_in_dim | solution.py:481
  181.0 0.0 copy-start
  181.0 0.0 copy-done.2
  181.0 0.0 copy-done.5
  181.0 0.0 copy-done.6
  181.0 0.0 copy-done.7
  181.1 2.0 %fusion.5 = (f32[1,1536,128]{2,1,0:T(8,128)}, f32[1,1536,128]{2,1,0:T(8,128)}, f32[1,1536,128]{2,1,0:T(8,128)}) fusion(f32[1536,128]{1,0:T(8,128)S(1)} %copy-done.7, f32[]{:T(128)S(6)} %div.33, f32[1,1536,128]{2,1,0:T(8,128)S(1)} %copy-done.5, f32[1,1536,128]{2,1,0:T(8,128)S(1)} %copy-done.6, f32[1,1536,128]{2,1,0:T(8,128)S(1)} %copy-done.2), kind=kLoop, calls=%fused_computation.11 | loop fusion | flops 3145728 | bytes 5505028 | tf_op jit(solution)/shard_map/broadcast_in_dim | solution.py:480
  183.1 0.6 copy-done
  183.6 1.7 copy.17
Async XLA Ops:
  0.6 177.1 %copy-start.1 = (f32[1,128,1536]{2,1,0:T(8,128)S(1)}, f32[1,128,1536]{2,1,0:T(8,128)}, u32[]{:S(2)}) copy-start(f32[1,128,1536]{2,1,0:T(8,128)} %param.13) | copy-start | bytes 2359300
  0.6 177.1 %copy-start.3 = (f32[1,128,1536]{2,1,0:T(8,128)S(1)}, f32[1,128,1536]{2,1,0:T(8,128)}, u32[]{:S(2)}) copy-start(f32[1,128,1536]{2,1,0:T(8,128)} %param.17) | copy-start | bytes 2359300
  0.7 177.1 %copy-start.4 = (f32[1,128,1536]{2,1,0:T(8,128)S(1)}, f32[1,128,1536]{2,1,0:T(8,128)}, u32[]{:S(2)}) copy-start(f32[1,128,1536]{2,1,0:T(8,128)} %param.15) | copy-start | bytes 2359300
  175.6 5.5 %copy-start.2 = (f32[1,1536,128]{2,1,0:T(8,128)S(1)}, f32[1,1536,128]{2,1,0:T(8,128)}, u32[]{:S(2)}) copy-start(f32[1,1536,128]{2,1,0:T(8,128)} %param.12) | copy-start | bytes 2359300
  177.7 3.4 %copy-start.5 = (f32[1,1536,128]{2,1,0:T(8,128)S(1)}, f32[1,1536,128]{2,1,0:T(8,128)}, u32[]{:S(2)}) copy-start(f32[1,1536,128]{2,1,0:T(8,128)} %param.16) | copy-start | bytes 2359300
  177.7 3.4 %copy-start.6 = (f32[1,1536,128]{2,1,0:T(8,128)S(1)}, f32[1,1536,128]{2,1,0:T(8,128)}, u32[]{:S(2)}) copy-start(f32[1,1536,128]{2,1,0:T(8,128)} %param.14) | copy-start | bytes 2359300
  177.7 3.4 %copy-start.7 = (f32[1536,128]{1,0:T(8,128)S(1)}, f32[1536,128]{1,0:T(8,128)}, u32[]{:S(2)}) copy-start(f32[1536,128]{1,0:T(8,128)} %get-tuple-element.13) | copy-start | bytes 2359300
  181.0 2.6 %copy-start = (bf16[128,12288]{1,0:T(8,128)(2,1)S(1)}, bf16[128,12288]{1,0:T(8,128)(2,1)}, u32[]{:S(2)}) copy-start(bf16[128,12288]{1,0:T(8,128)(2,1)} %get-tuple-element.11) | copy-start | bytes 9437188
